TPU v7x, 32 devices: a whole 2x2x4 slice. The times are simulated.
32 devices in a mesh: ctx: 4 (over z), exp: 8 (over y, x, core).
Axes of the slice: x: 2, y: 2, z: 4, core: 2. Of those that a mesh axis runs over, the one named last changes fastest.
Arguments:
- queries: bfloat16 [1024, 4096], P('ctx', 'exp'), may hold values from -6 to 6
- keys: bfloat16 [1024, 256], P('ctx'), may hold values from -6 to 6
- values: bfloat16 [1024, 256], P('ctx'), may hold values from -6 to 6
- attn_out: bfloat16 [1024, 4096], P('ctx', 'exp'), may hold values from -0.59765625 to 0.59765625
- attn_out_grad: bfloat16 [1024, 4096], P('ctx', 'exp'), may hold values from -6 to 6
- lse_excess: float32 [32, 1024], P('exp', 'ctx'), may hold values from 1 to 2.5
- block_mask: int32 [4, 4], replicated, may hold values from 0 to 1, as said below
- expert_ids: int32 [1024, 8], P('exp'), may hold values from 0 to 15, all different within a row; in each aligned block of 128 rows (0 to 127, 128 to 255, ...) at most 65 rows name the same one
- route_probs: bfloat16 [1024, 8], P('exp'), may hold values from 0.019897461 to 0.5
- moe_grad: bfloat16 [1024, 4096], P('exp'), may hold values from -6 to 6
- shadow_list: int32 [16], replicated, may hold values from -1 to 7, as said below
- stored_hidden_state: bfloat16 [8, 3, 8, 65, 1536], P('exp', None, None, None, 'ctx'), may hold values from -6 to 6
Outputs:
- query_grad: bfloat16 [1024, 4096], P('ctx', 'exp')
- key_grad: bfloat16 [1024, 256], P(('ctx', 'exp'))
- value_grad: bfloat16 [1024, 256], P(('ctx', 'exp'))
- expert_grad: float32 [16, 1536, 4096], P('exp', 'ctx')
Inputs may be any that keep to these rules, and one draw needn't show every extreme that they name: block_mask[i, j] is 1 on the diagonal and 0 above it. `expert_ids`: each token names 8 different experts; among the tokens of one exp index no expert is named more than 65 times, a bound that some block reaches. `shadow_list`: every exp index holds the shadow of exactly one expert, never of one it owns, and exactly one of the 2 experts of each exp index has a shadow.
All inputs are finite; a program needn't handle non-finite values.
Results may differ from a plain program's by a relative error of at most 0.015.
Values may be sent and summed in bfloat16 or wider, within the bound.
No kernel may reach another device: no remote copies, remote signals or barrier semaphores. Data moves between devices by JAX's collectives and lax.ppermute only.
A program may use at most 192 MiB of HBM per device.

v0:
```python
import math

import jax
import jax.numpy as jnp
from jax import lax
from jax.sharding import PartitionSpec as P


def passed_along(value, axis, steps):
    count = lax.axis_size(axis)
    pairs = [(source, (source + steps) % count) for source in range(count)]
    return lax.ppermute(value, axis, pairs)


def pair_terms(query_heads, grad_heads, delta, offset, key_block, value_block, diagonal):
    rows = query_heads.shape[0]
    scale = 1.0 / math.sqrt(query_heads.shape[2])
    scores = (
        jnp.einsum("qhd,kd->hqk", query_heads, key_block, preferred_element_type=jnp.float32)
        * scale
    )
    place = jnp.arange(rows, dtype=jnp.int32)
    allowed = jnp.logical_or(jnp.logical_not(diagonal), place[:, None] >= place[None, :])
    prob = jnp.where(allowed[None], jnp.exp(scores - offset[:, :, None]), 0.0)
    prob_low = prob.astype(jnp.bfloat16)
    value_term = jnp.einsum("hqk,qhd->kd", prob_low, grad_heads, preferred_element_type=jnp.float32)
    prob_grad = jnp.einsum(
        "qhd,kd->hqk", grad_heads, value_block, preferred_element_type=jnp.float32
    )
    score_grad = (prob * (prob_grad - delta[:, :, None]) * scale).astype(jnp.bfloat16)
    query_term = jnp.einsum(
        "hqk,kd->qhd", score_grad, key_block, preferred_element_type=jnp.float32
    )
    key_term = jnp.einsum(
        "hqk,qhd->kd", score_grad, query_heads, preferred_element_type=jnp.float32
    )
    return (query_term, key_term, value_term)


def attention(queries, keys, values, attn_out, attn_out_grad, lse_excess, block_mask):
    rows = queries.shape[0]
    heads = lse_excess.shape[0]
    width = queries.shape[1] // heads
    cycle = lax.axis_size("ctx")
    mine = lax.axis_index("ctx")
    owners = lax.axis_size("exp")
    kv_count = keys.shape[1] // width
    kv_head = lax.axis_index("exp") * kv_count // owners
    key_block = lax.dynamic_slice_in_dim(keys, kv_head * width, width, 1)
    value_block = lax.dynamic_slice_in_dim(values, kv_head * width, width, 1)
    query_heads = queries.reshape(rows, heads, width)
    grad_heads = attn_out_grad.reshape(rows, heads, width)
    delta = jnp.einsum(
        "qhd,qhd->hq",
        grad_heads,
        attn_out.reshape(rows, heads, width),
        preferred_element_type=jnp.float32,
    )
    offset = 0.5 * math.log(rows) + lse_excess
    zero_query = jnp.zeros((rows, heads, width), jnp.float32)
    zero_pair = jnp.zeros((rows, width), jnp.float32)

    def visit(step, carry):
        key_now, value_now, key_sum, value_sum, query_sum = carry
        source = (mine - step) % cycle
        live = block_mask[mine, source] > 0
        terms = lax.cond(
            live,
            lambda: pair_terms(
                query_heads, grad_heads, delta, offset, key_now, value_now, source == mine
            ),
            lambda: (zero_query, zero_pair, zero_pair),
        )
        key_sum = (key_sum.astype(jnp.float32) + terms[1]).astype(jnp.bfloat16)
        value_sum = (value_sum.astype(jnp.float32) + terms[2]).astype(jnp.bfloat16)
        query_sum = query_sum + terms[0]
        key_now, value_now, key_sum, value_sum = passed_along(
            (key_now, value_now, key_sum, value_sum), "ctx", 1
        )
        return (key_now, value_now, key_sum, value_sum, query_sum)

    start = (
        key_block,
        value_block,
        jnp.zeros((rows, width), jnp.bfloat16),
        jnp.zeros((rows, width), jnp.bfloat16),
        zero_query,
    )
    _, _, key_sum, value_sum, query_sum = lax.fori_loop(0, cycle, visit, start)
    query_grad = query_sum.reshape(rows, heads * width).astype(jnp.bfloat16)
    pick = (jnp.arange(kv_count, dtype=jnp.int32) == kv_head).astype(jnp.float32)
    wide_key = (key_sum.astype(jnp.float32)[:, None, :] * pick[None, :, None]).reshape(
        rows, kv_count * width
    )
    wide_value = (value_sum.astype(jnp.float32)[:, None, :] * pick[None, :, None]).reshape(
        rows, kv_count * width
    )
    key_part, value_part = (
        lax.psum_scatter(
            wide_key.astype(jnp.bfloat16), "exp", scatter_dimension=0, tiled=True
        ).astype(jnp.float32),
        lax.psum_scatter(
            wide_value.astype(jnp.bfloat16), "exp", scatter_dimension=0, tiled=True
        ).astype(jnp.float32),
    )
    return (query_grad, key_part.astype(jnp.bfloat16), value_part.astype(jnp.bfloat16))


def route_slots(expert_ids, shadow_list, per_dev, capacity):
    tokens, top = expert_ids.shape
    count = tokens * top
    experts_all = shadow_list.shape[0]
    flat = expert_ids.reshape(count)
    table = flat[:, None] == jnp.arange(experts_all, dtype=jnp.int32)[None, :]
    shadow = jnp.sum(jnp.where(table, shadow_list[None, :], 0), axis=1)
    order = jnp.arange(count, dtype=jnp.int32)
    side = jnp.logical_and(shadow >= 0, order // top % 2 == 1)
    owner = flat // per_dev
    target_dev = jnp.where(side, shadow, owner)
    slot = jnp.where(side, per_dev, flat % per_dev)
    label = flat * 2 + side.astype(jnp.int32)
    earlier = jnp.logical_and(label[:, None] == label[None, :], order[:, None] > order[None, :])
    rank = jnp.sum(earlier.astype(jnp.int32), axis=1)
    return (target_dev * (per_dev + 1) + slot) * capacity + rank


def packed_rows(expert_ids, route_probs, moe_grad, destination, owners, slots, capacity):
    tokens, top = expert_ids.shape
    total = owners * slots * capacity
    place = jnp.arange(total, dtype=jnp.int32)[:, None] == destination[None, :]
    place_tok = jnp.sum(place.reshape(total, tokens, top).astype(jnp.int32), axis=2)
    rows_out = jnp.dot(
        place_tok.astype(jnp.bfloat16), moe_grad, preferred_element_type=jnp.float32
    ).astype(jnp.bfloat16)
    weight_out = jnp.dot(
        place.astype(jnp.bfloat16),
        route_probs.reshape(tokens * top, 1),
        preferred_element_type=jnp.float32,
    ).astype(jnp.bfloat16)
    return (
        rows_out.reshape(owners, slots, capacity, moe_grad.shape[1]),
        weight_out.reshape(owners, slots, capacity),
    )


def slot_tiles(hidden, rows_in, weight_in):
    scaled = hidden.astype(jnp.float32) * jnp.transpose(weight_in, (1, 0, 2))[..., None].astype(
        jnp.float32
    )
    weighted = scaled.astype(jnp.bfloat16)
    return jnp.einsum("ascf,sacd->afd", weighted, rows_in, preferred_element_type=jnp.float32)


def experts(expert_ids, route_probs, moe_grad, shadow_list, stored_hidden_state):
    owners = lax.axis_size("exp")
    own_index = lax.axis_index("exp")
    per_dev = shadow_list.shape[0] // owners
    slots = per_dev + 1
    capacity = stored_hidden_state.shape[3]
    hidden = stored_hidden_state[0]
    mine_list = lax.dynamic_slice_in_dim(shadow_list, own_index * per_dev, per_dev)
    flags = mine_list >= 0
    helper_dev = jnp.sum(jnp.where(flags, mine_list, 0))
    hosted = shadow_list == own_index
    host_owner = jnp.sum(
        jnp.where(hosted, jnp.arange(shadow_list.shape[0], dtype=jnp.int32) // per_dev, 0)
    )
    toward = jnp.arange(owners, dtype=jnp.int32) == host_owner
    destination = route_slots(expert_ids, shadow_list, per_dev, capacity)
    rows_out, weight_out = packed_rows(
        expert_ids, route_probs, moe_grad, destination, owners, slots, capacity
    )
    rows_in, weight_in = (
        lax.all_to_all(rows_out, "exp", split_axis=0, concat_axis=0, tiled=True),
        lax.all_to_all(weight_out, "exp", split_axis=0, concat_axis=0, tiled=True),
    )
    tiles = slot_tiles(hidden, rows_in, weight_in)
    helper_tile = tiles[per_dev].astype(jnp.bfloat16)
    outgoing = jnp.where(toward[:, None, None], helper_tile[None], jnp.zeros((), jnp.bfloat16))
    arrived_tiles = lax.all_to_all(outgoing, "exp", split_axis=0, concat_axis=0, tiled=True)
    returned = lax.dynamic_index_in_dim(arrived_tiles, helper_dev, 0, keepdims=False).astype(
        jnp.float32
    )
    own_tiles = tiles[:per_dev]
    return own_tiles + jnp.where(flags[:, None, None], returned[None], 0.0)


def local(
    queries,
    keys,
    values,
    attn_out,
    attn_out_grad,
    lse_excess,
    block_mask,
    expert_ids,
    route_probs,
    moe_grad,
    shadow_list,
    stored_hidden_state,
):
    query_grad, key_grad, value_grad = attention(
        queries, keys, values, attn_out, attn_out_grad, lse_excess, block_mask
    )
    expert_grad = experts(expert_ids, route_probs, moe_grad, shadow_list, stored_hidden_state)
    return (query_grad, key_grad, value_grad, expert_grad)


def solution(mesh):
    placed = (
        P("ctx", "exp"),
        P("ctx", None),
        P("ctx", None),
        P("ctx", "exp"),
        P("ctx", "exp"),
        P("exp", "ctx"),
        P(),
        P("exp", None),
        P("exp", None),
        P("exp", None),
        P(),
        P("exp", None, None, None, "ctx"),
    )
    return jax.shard_map(
        local,
        mesh=mesh,
        in_specs=placed,
        out_specs=(
            P("ctx", "exp"),
            P(("ctx", "exp"), None),
            P(("ctx", "exp"), None),
            P("exp", "ctx", None),
        ),
        check_vma=False,
    )
```

profile of v0, /device:TPU:0, one launch (start us, length us, event | category | flops | bytes accessed | tf_op | source)
XLA Modules:
  0.0 546.0 jit_solution(5102361396125747858)
XLA Ops:
  7.2 0.9 copy.71
  8.1 0.7 select_reduce_fusion
  9.5 0.8 copy.72
  10.4 1.2 fusion.26
  11.5 0.7 reshape.227
  12.2 5.2 all-to-all-start
  17.7 0.7 fusion.44
  18.4 8.1 %convert_reduce_fusion = s32[1560,128]{1,0:T(8,128)S(1)} fusion(s32[128,8]{0,1:T(8,128)S(1)} %fusion.44), kind=kLoop, calls=%fused_computation.28 | loop fusion | flops 4592640 | bytes 802816 | tf_op jit(solution)/shard_map/reduce_sum | solution.py:131
  26.6 6.5 %convolution_convert_fusion = bf16[1560,4096]{1,0:T(8,128)(2,1)} fusion(bf16[128,4096]{1,0:T(8,128)(2,1)S(1)} %copy-done, s32[1560,128]{1,0:T(8,128)S(1)} %convert_reduce_fusion), kind=kOutput, calls=%fused_computation.23 | convolution fusion | flops 1642368000 | bytes 14626816 | tf_op jit(solution)/shard_map/dot_general | solution.py:132
  33.0 17.1 %reshape.228 = bf16[8,3,65,4096]{3,2,1,0:T(8,128)(2,1)} reshape(bf16[1560,4096]{1,0:T(8,128)(2,1)} %convolution_convert_fusion) | data formatting | bytes 25559040 | tf_op jit(solution)/shard_map/reshape | solution.py:141
  50.1 5.8 %all-to-all-start.1 = ((bf16[8,3,65,4096]{3,2,1,0:T(8,128)(2,1)}), bf16[8,3,65,4096]{3,2,1,0:T(8,128)(2,1)}, u32[]{:S(2)}, u32[]{:S(2)}) async-start(bf16[8,3,65,4096]{3,2,1,0:T(8,128)(2,1)} %reshape.228), calls=%async_computation.3 | async-start | bytes 28311552 | tf_op jit(solution)/shard_map/all_to_all | solution.py:174
  56.6 1.2 iota_compare_fusion.8
  57.9 154.0 %all-to-all-done.1 = bf16[8,3,65,4096]{3,2,1,0:T(8,128)(2,1)} async-done(((bf16[8,3,65,4096]{3,2,1,0:T(8,128)(2,1)}), bf16[8,3,65,4096]{3,2,1,0:T(8,128)(2,1)}, u32[]{:S(2)}, u32[]{:S(2)}) %all-to-all-start.1) | async-done | bytes 12779552 | tf_op jit(solution)/shard_map/all_to_all | solution.py:174
  211.8 20.6 %fusion.15 = f32[3,384,4096]{2,1,0:T(8,128)} fusion(bf16[8,3,65,4096]{3,2,1,0:T(8,128)(2,1)} %all-to-all-done.1, bf16[1,3,8,65,384]{4,2,3,1,0:T(8,128)(2,1)S(1)} %copy-done.11, f32[3,8,65]{1,2,0:T(8,128)S(1)} %copy.73), kind=kOutput, calls=%fused_computation.27 | convolution fusion | flops 4909132800 | bytes 32858208 | tf_op jit(solution)/shard_map/ascf,sacd->afd/dot_general | solution.py:151
  232.5 3.2 fusion.21
  235.7 8.6 %broadcast_select_fusion = bf16[8,384,4096]{2,1,0:T(8,128)(2,1)} fusion(pred[8]{0:T(512)(128)(4,1)S(1)} %copy-done.10, bf16[384,4096]{1,0:T(8,128)(2,1)S(1)} %fusion.21), kind=kLoop, calls=%fused_computation.22 | loop fusion | flops 12582912 | bytes 28311560 | tf_op jit(solution)/shard_map/jit(_where)/select_n | solution.py:179
  244.3 6.6 %all-to-all-start.2 = ((bf16[8,384,4096]{2,1,0:T(8,128)(2,1)}), bf16[8,384,4096]{2,1,0:T(8,128)(2,1)}, u32[]{:S(2)}, u32[]{:S(2)}) async-start(bf16[8,384,4096]{2,1,0:T(8,128)(2,1)} %broadcast_select_fusion), calls=%async_computation.4 | async-start | bytes 50331648 | tf_op jit(solution)/shard_map/all_to_all | solution.py:180
  252.5 60.7 %while.24 = (s32[]{:T(128)}, bf16[256,128]{1,0:T(8,128)(2,1)S(1)}, bf16[256,128]{1,0:T(8,128)(2,1)S(1)}, bf16[256,128]{1,0:T(8,128)(2,1)S(1)}, bf16[256,128]{1,0...) while((s32[]{:T(128)}, bf16[256,128]{1,0:T(8,128)(2,1)S(1)}, ...), condition=%wide.region_3.4_spmd.clone, body=%wide.region_0.3_spmd.clone.sunk | while | flops 338231328 | bytes 10297960 | solution.py:89
  253.2 1.6 collective-permute-start
  255.4 1.6 collective-permute-start.1
  257.0 1.3 dynamic_slice.34
  258.9 4.2 conditional.3
  259.0 1.2 fusion.6
  260.2 1.1 fusion.7
  261.3 1.2 convolution_bitcast_fusion.1
  263.1 1.6 collective-permute-start.2
  265.2 4.6 collective-permute-done.2
  269.8 1.1 collective-permute-done.3
  272.2 1.3 dynamic_slice.34
  274.2 5.7 %collective-permute-start.2 = (bf16[256,128]{1,0:T(8,128)(2,1)S(1)}, bf16[256,128]{1,0:T(8,128)(2,1)S(1)}, u32[]{:S(2)}, u32[]{:S(2)}) collective-permute-start(bf16[256,128]{1,0:T(8,128)(2,1)S(1)} %add_convert_fusion.4), channel_id=1, source_target_pairs={{0,8},{8,16},{16,24},{24,0},{1,9},{9,17},{17,25},{25,1},{2,10},{10... | collective-permute-start | bytes 196616 | tf_op jit(solution)/shard_map/while/body/eval_jaxpr/ppermute | solution.py:12
  280.2 1.7 collective-permute-done.2
  281.8 4.2 collective-permute-done.3
  287.4 1.3 dynamic_slice.34
  289.4 0.8 collective-permute-start.2
  290.3 4.2 collective-permute-start.3
  294.6 5.0 collective-permute-done.2
  301.8 2.4 collective-permute-start.1
  304.1 1.3 dynamic_slice.34
  306.2 1.0 collective-permute-start.2
  307.2 1.6 collective-permute-start.3
  308.9 3.4 collective-permute-done.2
  312.3 1.0 collective-permute-done.3
  313.4 0.7 fusion.28
  315.0 0.7 select_reduce_fusion.1
  317.7 0.7 copy_bitcast_fusion
  318.4 207.4 %all-to-all-done.2 = bf16[8,384,4096]{2,1,0:T(8,128)(2,1)} async-done(((bf16[8,384,4096]{2,1,0:T(8,128)(2,1)}), bf16[8,384,4096]{2,1,0:T(8,128)(2,1)}, u32[]{:S(2)}, u32[]{:S(2)}) %all-to-all-start.2) | async-done | bytes 25165856 | tf_op jit(solution)/shard_map/all_to_all | solution.py:180
  525.8 2.6 bitcast_convert_fusion
  528.4 10.7 %slice_add_fusion = f32[2,384,4096]{2,1,0:T(8,128)} fusion(f32[3,384,4096]{2,1,0:T(8,128)} %fusion.15, f32[384,4096]{1,0:T(8,128)S(1)} %bitcast_convert_fusion, pred[2]{0:T(512)(128)(4,1)S(1)} %broadcast_compare_fusion), kind=kLoop, calls=%fused_computation.26 | loop fusion | flops 6291456 | bytes 31457282 | tf_op jit(solution)/shard_map/add | solution.py:185
  (112 shorter events, 12.3 us)
Async XLA Ops:
  7.2 19.4 %copy-start = (bf16[128,4096]{1,0:T(8,128)(2,1)S(1)}, bf16[128,4096]{1,0:T(8,128)(2,1)}, u32[]{:S(2)}) copy-start(bf16[128,4096]{1,0:T(8,128)(2,1)} %param.25) | copy-start | bytes 3145732
  12.2 37.9 %all-to-all-start = ((bf16[8,3,65]{2,1,0:T(4,128)(2,1)}), bf16[8,3,65]{2,1,0:T(4,128)(2,1)S(1)}, u32[]{:S(2)}, u32[]{:S(2)}) async-start(bf16[8,3,65]{2,1,0:T(4,128)(2,1)} %reshape.227), calls=%async_computation.2 | async-start | bytes 16384 | tf_op jit(solution)/shard_map/all_to_all | solution.py:175
  50.1 5.8 %copy-start.8 = (s32[16]{0:T(128)S(1)}, s32[16]{0:T(128)}, u32[]{:S(2)}) copy-start(s32[16]{0:T(128)} %param.26) | copy-start | bytes 196
  50.1 161.7 %copy-start.11 = (bf16[1,3,8,65,384]{4,2,3,1,0:T(8,128)(2,1)S(1)}, bf16[1,3,8,65,384]{4,2,3,1,0:T(8,128)(2,1)}, u32[]{:S(2)}) copy-start(bf16[1,3,8,65,384]{4,2,3,1,0:T(8,128)(2,1)} %param.27) | copy-start | bytes 3594244
  50.1 161.7 %all-to-all-start.1 = ((bf16[8,3,65,4096]{3,2,1,0:T(8,128)(2,1)}), bf16[8,3,65,4096]{3,2,1,0:T(8,128)(2,1)}, u32[]{:S(2)}, u32[]{:S(2)}) async-start(bf16[8,3,65,4096]{3,2,1,0:T(8,128)(2,1)} %reshape.228), calls=%async_computation.3 | async-start | bytes 28311552 | tf_op jit(solution)/shard_map/all_to_all | solution.py:174
  211.8 23.9 %copy-start.10 = (pred[8]{0:T(512)(128)(4,1)S(1)}, pred[8]{0:T(512)(128)(4,1)}, u32[]{:S(2)}) copy-start(pred[8]{0:T(512)(128)(4,1)} %iota_compare_fusion.8) | copy-start | bytes 28
  244.3 6.7 %copy-start.2 = (bf16[256,512]{1,0:T(8,128)(2,1)S(1)}, bf16[256,512]{1,0:T(8,128)(2,1)}, u32[]{:S(2)}) copy-start(bf16[256,512]{1,0:T(8,128)(2,1)} %param.20) | copy-start | bytes 786436
  244.3 7.0 %copy-start.3 = (bf16[256,512]{1,0:T(8,128)(2,1)S(1)}, bf16[256,512]{1,0:T(8,128)(2,1)}, u32[]{:S(2)}) copy-start(bf16[256,512]{1,0:T(8,128)(2,1)} %param.19) | copy-start | bytes 786436
  244.3 7.7 %copy-start.4 = (bf16[256,512]{1,0:T(8,128)(2,1)S(1)}, bf16[256,512]{1,0:T(8,128)(2,1)}, u32[]{:S(2)}) copy-start(bf16[256,512]{1,0:T(8,128)(2,1)} %param.16) | copy-start | bytes 786436
  244.3 8.1 %copy-start.5 = (bf16[256,256]{1,0:T(8,128)(2,1)S(1)}, bf16[256,256]{1,0:T(8,128)(2,1)}, u32[]{:S(2)}) copy-start(bf16[256,256]{1,0:T(8,128)(2,1)} %param.18) | copy-start | bytes 393220
  244.3 8.1 %copy-start.6 = (bf16[256,256]{1,0:T(8,128)(2,1)S(1)}, bf16[256,256]{1,0:T(8,128)(2,1)}, u32[]{:S(2)}) copy-start(bf16[256,256]{1,0:T(8,128)(2,1)} %param.17) | copy-start | bytes 393220
  244.3 8.2 %copy-start.7 = (f32[4,256]{1,0:T(4,128)S(1)}, f32[4,256]{1,0:T(4,128)}, u32[]{:S(2)}) copy-start(f32[4,256]{1,0:T(4,128)} %param.21) | copy-start | bytes 12292
  244.3 281.5 %all-to-all-start.2 = ((bf16[8,384,4096]{2,1,0:T(8,128)(2,1)}), bf16[8,384,4096]{2,1,0:T(8,128)(2,1)}, u32[]{:S(2)}, u32[]{:S(2)}) async-start(bf16[8,384,4096]{2,1,0:T(8,128)(2,1)} %broadcast_select_fusion), calls=%async_computation.4 | async-start | bytes 50331648 | tf_op jit(solution)/shard_map/all_to_all | solution.py:180
  250.9 288.2 %reduce-scatter.3.cloned.1.call-start = ((), (), s32[]{:S(2)}) async-start(), calls=%async_computation.5 | async-start | bytes 147456 | tf_op jit(solution)/shard_map/reduce_scatter | solution.py:99
  252.5 62.4 %copy-start.9 = (s32[16]{0:T(128)S(1)}, s32[16]{0:T(128)}, u32[]{:S(2)}) copy-start(s32[16]{0:T(128)} %param.26) | copy-start | bytes 196
  253.2 17.7 %collective-permute-start = (bf16[256,128]{1,0:T(8,128)(2,1)}, bf16[256,128]{1,0:T(8,128)(2,1)S(1)}, u32[]{:S(2)}, u32[]{:S(2)}) collective-permute-start(bf16[256,128]{1,0:T(8,128)(2,1)} %copy.111), channel_id=1, source_target_pairs={{0,8},{8,16},{16,24},{24,0},{1,9},{9,17},{17,25},{25,1},{2,10},{10... | collective-permute-start | bytes 196616 | tf_op jit(solution)/shard_map/while/body/eval_jaxpr/ppermute | solution.py:12
  255.4 15.5 %collective-permute-start.1 = (bf16[256,128]{1,0:T(8,128)(2,1)}, bf16[256,128]{1,0:T(8,128)(2,1)S(1)}, u32[]{:S(2)}, u32[]{:S(2)}) collective-permute-start(bf16[256,128]{1,0:T(8,128)(2,1)} %copy.112), channel_id=1, source_target_pairs={{0,8},{8,16},{16,24},{24,0},{1,9},{9,17},{17,25},{25,1},{2,10},{10... | collective-permute-start | bytes 196616 | tf_op jit(solution)/shard_map/while/body/eval_jaxpr/ppermute | solution.py:12
  263.1 6.7 %collective-permute-start.2 = (bf16[256,128]{1,0:T(8,128)(2,1)S(1)}, bf16[256,128]{1,0:T(8,128)(2,1)S(1)}, u32[]{:S(2)}, u32[]{:S(2)}) collective-permute-start(bf16[256,128]{1,0:T(8,128)(2,1)S(1)} %add_convert_fusion.4), channel_id=1, source_target_pairs={{0,8},{8,16},{16,24},{24,0},{1,9},{9,17},{17,25},{25,1},{2,10},{10... | collective-permute-start | bytes 196616 | tf_op jit(solution)/shard_map/while/body/eval_jaxpr/ppermute | solution.py:12
  264.8 6.1 %collective-permute-start.3 = (bf16[256,128]{1,0:T(8,128)(2,1)S(1)}, bf16[256,128]{1,0:T(8,128)(2,1)S(1)}, u32[]{:S(2)}, u32[]{:S(2)}) collective-permute-start(bf16[256,128]{1,0:T(8,128)(2,1)S(1)} %add_convert_fusion.5), channel_id=1, source_target_pairs={{0,8},{8,16},{16,24},{24,0},{1,9},{9,17},{17,25},{25,1},{2,10},{10... | collective-permute-start | bytes 196616 | tf_op jit(solution)/shard_map/while/body/eval_jaxpr/ppermute | solution.py:12
  271.5 14.6 %collective-permute-start = (bf16[256,128]{1,0:T(8,128)(2,1)}, bf16[256,128]{1,0:T(8,128)(2,1)S(1)}, u32[]{:S(2)}, u32[]{:S(2)}) collective-permute-start(bf16[256,128]{1,0:T(8,128)(2,1)} %copy.111), channel_id=1, source_target_pairs={{0,8},{8,16},{16,24},{24,0},{1,9},{9,17},{17,25},{25,1},{2,10},{10... | collective-permute-start | bytes 196616 | tf_op jit(solution)/shard_map/while/body/eval_jaxpr/ppermute | solution.py:12
  272.1 13.9 %collective-permute-start.1 = (bf16[256,128]{1,0:T(8,128)(2,1)}, bf16[256,128]{1,0:T(8,128)(2,1)S(1)}, u32[]{:S(2)}, u32[]{:S(2)}) collective-permute-start(bf16[256,128]{1,0:T(8,128)(2,1)} %copy.112), channel_id=1, source_target_pairs={{0,8},{8,16},{16,24},{24,0},{1,9},{9,17},{17,25},{25,1},{2,10},{10... | collective-permute-start | bytes 196616 | tf_op jit(solution)/shard_map/while/body/eval_jaxpr/ppermute | solution.py:12
  274.2 7.6 %collective-permute-start.2 = (bf16[256,128]{1,0:T(8,128)(2,1)S(1)}, bf16[256,128]{1,0:T(8,128)(2,1)S(1)}, u32[]{:S(2)}, u32[]{:S(2)}) collective-permute-start(bf16[256,128]{1,0:T(8,128)(2,1)S(1)} %add_convert_fusion.4), channel_id=1, source_target_pairs={{0,8},{8,16},{16,24},{24,0},{1,9},{9,17},{17,25},{25,1},{2,10},{10... | collective-permute-start | bytes 196616 | tf_op jit(solution)/shard_map/while/body/eval_jaxpr/ppermute | solution.py:12
  280.0 6.1 %collective-permute-start.3 = (bf16[256,128]{1,0:T(8,128)(2,1)S(1)}, bf16[256,128]{1,0:T(8,128)(2,1)S(1)}, u32[]{:S(2)}, u32[]{:S(2)}) collective-permute-start(bf16[256,128]{1,0:T(8,128)(2,1)S(1)} %add_convert_fusion.5), channel_id=1, source_target_pairs={{0,8},{8,16},{16,24},{24,0},{1,9},{9,17},{17,25},{25,1},{2,10},{10... | collective-permute-start | bytes 196616 | tf_op jit(solution)/shard_map/while/body/eval_jaxpr/ppermute | solution.py:12
  286.7 13.6 %collective-permute-start = (bf16[256,128]{1,0:T(8,128)(2,1)}, bf16[256,128]{1,0:T(8,128)(2,1)S(1)}, u32[]{:S(2)}, u32[]{:S(2)}) collective-permute-start(bf16[256,128]{1,0:T(8,128)(2,1)} %copy.111), channel_id=1, source_target_pairs={{0,8},{8,16},{16,24},{24,0},{1,9},{9,17},{17,25},{25,1},{2,10},{10... | collective-permute-start | bytes 196616 | tf_op jit(solution)/shard_map/while/body/eval_jaxpr/ppermute | solution.py:12
  287.3 13.0 %collective-permute-start.1 = (bf16[256,128]{1,0:T(8,128)(2,1)}, bf16[256,128]{1,0:T(8,128)(2,1)S(1)}, u32[]{:S(2)}, u32[]{:S(2)}) collective-permute-start(bf16[256,128]{1,0:T(8,128)(2,1)} %copy.112), channel_id=1, source_target_pairs={{0,8},{8,16},{16,24},{24,0},{1,9},{9,17},{17,25},{25,1},{2,10},{10... | collective-permute-start | bytes 196616 | tf_op jit(solution)/shard_map/while/body/eval_jaxpr/ppermute | solution.py:12
  289.4 10.2 %collective-permute-start.2 = (bf16[256,128]{1,0:T(8,128)(2,1)S(1)}, bf16[256,128]{1,0:T(8,128)(2,1)S(1)}, u32[]{:S(2)}, u32[]{:S(2)}) collective-permute-start(bf16[256,128]{1,0:T(8,128)(2,1)S(1)} %add_convert_fusion.4), channel_id=1, source_target_pairs={{0,8},{8,16},{16,24},{24,0},{1,9},{9,17},{17,25},{25,1},{2,10},{10... | collective-permute-start | bytes 196616 | tf_op jit(solution)/shard_map/while/body/eval_jaxpr/ppermute | solution.py:12
  290.3 10.1 %collective-permute-start.3 = (bf16[256,128]{1,0:T(8,128)(2,1)S(1)}, bf16[256,128]{1,0:T(8,128)(2,1)S(1)}, u32[]{:S(2)}, u32[]{:S(2)}) collective-permute-start(bf16[256,128]{1,0:T(8,128)(2,1)S(1)} %add_convert_fusion.5), channel_id=1, source_target_pairs={{0,8},{8,16},{16,24},{24,0},{1,9},{9,17},{17,25},{25,1},{2,10},{10... | collective-permute-start | bytes 196616 | tf_op jit(solution)/shard_map/while/body/eval_jaxpr/ppermute | solution.py:12
  301.0 12.3 %collective-permute-start = (bf16[256,128]{1,0:T(8,128)(2,1)}, bf16[256,128]{1,0:T(8,128)(2,1)S(1)}, u32[]{:S(2)}, u32[]{:S(2)}) collective-permute-start(bf16[256,128]{1,0:T(8,128)(2,1)} %copy.111), channel_id=1, source_target_pairs={{0,8},{8,16},{16,24},{24,0},{1,9},{9,17},{17,25},{25,1},{2,10},{10... | collective-permute-start | bytes 196616 | tf_op jit(solution)/shard_map/while/body/eval_jaxpr/ppermute | solution.py:12
  301.8 11.5 %collective-permute-start.1 = (bf16[256,128]{1,0:T(8,128)(2,1)}, bf16[256,128]{1,0:T(8,128)(2,1)S(1)}, u32[]{:S(2)}, u32[]{:S(2)}) collective-permute-start(bf16[256,128]{1,0:T(8,128)(2,1)} %copy.112), channel_id=1, source_target_pairs={{0,8},{8,16},{16,24},{24,0},{1,9},{9,17},{17,25},{25,1},{2,10},{10... | collective-permute-start | bytes 196616 | tf_op jit(solution)/shard_map/while/body/eval_jaxpr/ppermute | solution.py:12
  306.2 6.1 %collective-permute-start.2 = (bf16[256,128]{1,0:T(8,128)(2,1)S(1)}, bf16[256,128]{1,0:T(8,128)(2,1)S(1)}, u32[]{:S(2)}, u32[]{:S(2)}) collective-permute-start(bf16[256,128]{1,0:T(8,128)(2,1)S(1)} %add_convert_fusion.4), channel_id=1, source_target_pairs={{0,8},{8,16},{16,24},{24,0},{1,9},{9,17},{17,25},{25,1},{2,10},{10... | collective-permute-start | bytes 196616 | tf_op jit(solution)/shard_map/while/body/eval_jaxpr/ppermute | solution.py:12
  307.2 6.1 %collective-permute-start.3 = (bf16[256,128]{1,0:T(8,128)(2,1)S(1)}, bf16[256,128]{1,0:T(8,128)(2,1)S(1)}, u32[]{:S(2)}, u32[]{:S(2)}) collective-permute-start(bf16[256,128]{1,0:T(8,128)(2,1)S(1)} %add_convert_fusion.5), channel_id=1, source_target_pairs={{0,8},{8,16},{16,24},{24,0},{1,9},{9,17},{17,25},{25,1},{2,10},{10... | collective-permute-start | bytes 196616 | tf_op jit(solution)/shard_map/while/body/eval_jaxpr/ppermute | solution.py:12
  314.2 224.9 %reduce-scatter.5.cloned.1.call-start = ((), (), s32[]{:S(2)}) async-start(), calls=%async_computation.6 | async-start | bytes 147456 | tf_op jit(solution)/shard_map/reduce_scatter | solution.py:102
  528.4 10.7 %copy-start.1 = (bf16[128,4096]{1,0:T(8,128)(2,1)S(1)}, bf16[128,4096]{1,0:T(8,128)(2,1)}, u32[]{:S(2)}) copy-start(bf16[128,4096]{1,0:T(8,128)(2,1)} %param.25) | copy-start | bytes 3145732
Sparse Core Ops, SparseCore 0:
  314.3 86.1 reduce-scatter.2
  404.4 91.9 reduce-scatter.4
where the time goes:
time: 547 us; the launch traced here: 546 us
  waiting for transfers between devices  384 us (70%)
  starting transfers between devices  38.6 us (7%)
  other arithmetic  37.2 us (7%)
  local copies, waits for them, and re-layouts  34.9 us (6%)
  matrix products  32.4 us (6%)
  between operations  16.3 us (3%)
    all_to_all x1, waiting for transfers between devices, experts(): lax.all_to_all(outgoing, 'exp', split_axis=0, concat_axis=0, tiled=True)  207 us
    all_to_all x1, waiting for transfers between devices, experts(): lax.all_to_all(rows_out, 'exp', split_axis=0, concat_axis=0, tiled=True)  154 us
    ppermute x16, waiting for transfers between devices, passed_along(): return lax.ppermute(value, axis, pairs)  21.7 us
    ppermute x16, starting transfers between devices, passed_along(): return lax.ppermute(value, axis, pairs)  21 us
    dot_general x1, matrix products, slot_tiles(): jnp.einsum('ascf,sacd->afd', weighted, rows_in, preferred_element_type=jn...  20.6 us
    reshape x1, local copies, waits for them, and re-layouts, packed_rows(): rows_out.reshape(owners, slots, capacity, moe_grad.shape[1])  17.1 us
  transfers between devices with their start and end apart: 21, of which 10 were waited for; matrix products, arithmetic and copies ran while one was open for 12% of the time, Pallas kernels for 0%

commit v1 on v0

v1 whole, which is shorter than its diff:
```python
import functools
import math

import jax
import jax.numpy as jnp
from jax import lax
from jax.experimental import pallas as pl
from jax.experimental.pallas import tpu as pltpu
from jax.sharding import PartitionSpec as P

LAST = (((1,), (1,)), ((), ()))
FIRST = (((0,), (0,)), ((), ()))


def attention_kernel(
    live_ref, query_ref, grad_ref, out_ref, lse_ref, pairs_ref, query_grad_ref, terms_ref, sums_ref
):
    rows, width = pairs_ref.shape[1], pairs_ref.shape[2] // 2
    heads = lse_ref.shape[0]
    scale = 1.0 / math.sqrt(width)
    offset = 0.5 * math.log(rows) + lse_ref[...]
    spans = [slice(h * width, (h + 1) * width) for h in range(heads)]
    delta = []
    for span in spans:
        both = grad_ref[:, span].astype(jnp.float32) * out_ref[:, span].astype(jnp.float32)
        delta.append(jnp.sum(both.T, axis=0, keepdims=True))

    def block(step, diagonal):
        key, value = pairs_ref[step, :, :width], pairs_ref[step, :, width:]
        probs, slopes = [], []
        for h, span in enumerate(spans):
            query, grad = query_ref[:, span], grad_ref[:, span]
            scores = lax.dot_general(key, query, LAST, preferred_element_type=jnp.float32)
            prob = jnp.exp(scores * scale - offset[h : h + 1])
            if diagonal:
                at_key = lax.broadcasted_iota(jnp.int32, (rows, rows), 0)
                at_query = lax.broadcasted_iota(jnp.int32, (rows, rows), 1)
                prob = jnp.where(at_key <= at_query, prob, 0.0)
            prob_grad = lax.dot_general(value, grad, LAST, preferred_element_type=jnp.float32)
            slope = (prob * (prob_grad - delta[h]) * scale).astype(jnp.bfloat16)
            probs.append(prob.astype(jnp.bfloat16))
            slopes.append(slope)
            query_term = lax.dot_general(slope, key, FIRST, preferred_element_type=jnp.float32)
            if diagonal:
                sums_ref[:, span] = query_term
            else:
                sums_ref[:, span] += query_term
        queries = jnp.concatenate([query_ref[:, span] for span in spans], axis=0)
        grads = jnp.concatenate([grad_ref[:, span] for span in spans], axis=0)
        terms_ref[step, :, :width] = jnp.dot(
            jnp.concatenate(slopes, axis=1), queries, preferred_element_type=jnp.float32
        ).astype(jnp.bfloat16)
        terms_ref[step, :, width:] = jnp.dot(
            jnp.concatenate(probs, axis=1), grads, preferred_element_type=jnp.float32
        ).astype(jnp.bfloat16)

    block(0, True)

    @pl.loop(1, pairs_ref.shape[0])
    def _(step):
        @pl.when(live_ref[step] > 0)
        def _():
            block(step, False)

        @pl.when(live_ref[step] <= 0)
        def _():
            terms_ref[step] = jnp.zeros_like(terms_ref[step])

    query_grad_ref[...] = sums_ref[...].astype(jnp.bfloat16)


def attention(queries, keys, values, attn_out, attn_out_grad, lse_excess, block_mask):
    rows = queries.shape[0]
    heads = lse_excess.shape[0]
    width = queries.shape[1] // heads
    cycle = lax.axis_size("ctx")
    mine = lax.axis_index("ctx")
    owners = lax.axis_size("exp")
    kv_count = keys.shape[1] // width
    kv_head = lax.axis_index("exp") * kv_count // owners
    pair = jnp.concatenate(
        [
            lax.dynamic_slice_in_dim(keys, kv_head * width, width, 1),
            lax.dynamic_slice_in_dim(values, kv_head * width, width, 1),
        ],
        axis=1,
    )
    arrived = [pair] + [
        lax.ppermute(pair, "ctx", [(c, c + step) for c in range(cycle - step)])
        for step in range(1, cycle)
    ]
    source = mine - jnp.arange(cycle, dtype=jnp.int32)
    live = jnp.where(source >= 0, block_mask[mine, jnp.maximum(source, 0)], 0)
    whole = pl.BlockSpec(memory_space=pltpu.VMEM)
    query_grad, terms = pl.pallas_call(
        attention_kernel,
        out_shape=(
            jax.ShapeDtypeStruct(queries.shape, jnp.bfloat16),
            jax.ShapeDtypeStruct((cycle, rows, 2 * width), jnp.bfloat16),
        ),
        in_specs=[pl.BlockSpec(memory_space=pltpu.SMEM)] + [whole] * 5,
        out_specs=(whole, whole),
        scratch_shapes=[pltpu.VMEM(queries.shape, jnp.float32)],
        compiler_params=pltpu.CompilerParams(vmem_limit_bytes=40 * 2**20),
        name="attention",
    )(live, queries, attn_out_grad, attn_out, lse_excess, jnp.stack(arrived))
    total = terms[0].astype(jnp.float32)
    for step in range(1, cycle):
        total = total + lax.ppermute(
            terms[step], "ctx", [(c, c - step) for c in range(step, cycle)]
        ).astype(jnp.float32)
    parts = lax.all_to_all(
        total.astype(jnp.bfloat16), "exp", split_axis=0, concat_axis=0, tiled=True
    )
    kv_sum = jnp.sum(
        parts.reshape(kv_count, owners // kv_count, rows // owners, 2, width).astype(jnp.float32),
        axis=1,
    )
    final = jnp.transpose(kv_sum, (2, 1, 0, 3)).reshape(2, rows // owners, kv_count * width)
    final = final.astype(jnp.bfloat16)
    return (query_grad, final[0], final[1])


def rows_of_pairs(named, capacity):
    tokens = named.shape[-1]
    ones = named.astype(jnp.bfloat16)
    before = (
        lax.broadcasted_iota(jnp.int32, (tokens, tokens), 0)
        < lax.broadcasted_iota(jnp.int32, (tokens, tokens), 1)
    ).astype(jnp.bfloat16)
    rank = jnp.einsum("...u,ut->...t", ones, before, preferred_element_type=jnp.float32)
    place = jnp.arange(capacity, dtype=jnp.int32)
    return jnp.where(
        named[..., None] & (rank.astype(jnp.int32)[..., None] == place), 1.0, 0.0
    ).astype(jnp.bfloat16)


def experts(expert_ids, route_probs, moe_grad, shadow_list, stored_hidden_state):
    owners = lax.axis_size("exp")
    own_index = lax.axis_index("exp")
    tokens = expert_ids.shape[0]
    count = shadow_list.shape[0]
    per_dev = count // owners
    hidden = stored_hidden_state[0]
    units = hidden.shape[-1]
    swap = functools.partial(
        lax.all_to_all, axis_name="exp", split_axis=0, concat_axis=0, tiled=True
    )
    gathered = lax.all_gather(moe_grad, "exp", tiled=True)

    hit = expert_ids[:, None, :] == jnp.arange(count, dtype=jnp.int32)[None, :, None]
    table = jnp.sum(
        jnp.where(hit, route_probs[:, None, :].astype(jnp.float32), 0.0), axis=2
    ).astype(jnp.bfloat16)
    probs = swap(table.T).reshape(owners, per_dev, tokens)

    limit = min(hidden.shape[2], tokens // 2)
    by_source = swap(hidden[per_dev, :, :limit])
    hosts = jnp.max(shadow_list.reshape(owners, per_dev), axis=1)
    shadow_rows = swap(by_source[hosts])

    flags = lax.dynamic_slice_in_dim(shadow_list, own_index * per_dev, per_dev) >= 0
    odd = jnp.arange(tokens, dtype=jnp.int32) % 2 == 1
    named = probs > 0
    side = named & odd & flags[None, :, None]
    own_place = rows_of_pairs(named & ~side, hidden.shape[2])
    side_place = rows_of_pairs(side, limit)
    rows = jnp.einsum(
        "sjtr,jsrf->stjf", own_place, hidden[:per_dev], preferred_element_type=jnp.float32
    ) + jnp.einsum("sjtr,srf->stjf", side_place, shadow_rows, preferred_element_type=jnp.float32)
    weight = jnp.transpose(probs, (0, 2, 1))[..., None].astype(jnp.float32)
    weighted = (rows * weight).astype(jnp.bfloat16)
    tiles = lax.dot_general(
        weighted.reshape(owners * tokens, per_dev * units),
        gathered,
        FIRST,
        preferred_element_type=jnp.float32,
    )
    return tiles.reshape(per_dev, units, moe_grad.shape[1])


def local(
    queries,
    keys,
    values,
    attn_out,
    attn_out_grad,
    lse_excess,
    block_mask,
    expert_ids,
    route_probs,
    moe_grad,
    shadow_list,
    stored_hidden_state,
):
    query_grad, key_grad, value_grad = attention(
        queries, keys, values, attn_out, attn_out_grad, lse_excess, block_mask
    )
    expert_grad = experts(expert_ids, route_probs, moe_grad, shadow_list, stored_hidden_state)
    return (query_grad, key_grad, value_grad, expert_grad)


def solution(mesh):
    placed = (
        P("ctx", "exp"),
        P("ctx", None),
        P("ctx", None),
        P("ctx", "exp"),
        P("ctx", "exp"),
        P("exp", "ctx"),
        P(),
        P("exp", None),
        P("exp", None),
        P("exp", None),
        P(),
        P("exp", None, None, None, "ctx"),
    )
    return jax.shard_map(
        local,
        mesh=mesh,
        in_specs=placed,
        out_specs=(
            P("ctx", "exp"),
            P(("ctx", "exp"), None),
            P(("ctx", "exp"), None),
            P("exp", "ctx", None),
        ),
        check_vma=False,
    )
```

time: 547 us -> 108 us (0.20)
  waiting for transfers between devices: 384 us -> 20.6 us
  other arithmetic: 37.2 us -> 7.64 us
  local copies, waits for them, and re-layouts: 34.9 us -> 13.5 us
  matrix products: 32.4 us -> 15.9 us
  starting transfers between devices: 38.6 us -> 32 us
    all_to_all x3 -> x4, waiting for transfers between devices: 361 us -> 7.88 us  [the longest x1 5.64 us: attention(): lax.all_to_all(total.astype(jnp.bfloat16), 'exp', split_axis=0, concat_ax...]
    reshape x4 -> x1, local copies, waits for them, and re-layouts: 18 us -> 0.73 us  [experts(): hosts = jnp.max(shadow_list.reshape(owners, per_dev), axis=1)]
    dot_general x8 -> x5, matrix products: 32.4 us -> 15.9 us  [the longest x1 12.5 us: experts(): lax.dot_general(weighted.reshape(owners * tokens, per_dev * units), gathe...]
    add x9 -> x0, other arithmetic: 12.1 us -> none  [the longest x1 10.7 us: experts(): return own_tiles + jnp.where(flags[:, None, None], returned[None], 0.0)]
    ppermute x16 -> x6, waiting for transfers between devices: 21.7 us -> 12 us  [the longest x3 12 us: attention(): lax.ppermute(terms[step], 'ctx', [(c, c - step) for c in range(step, cycl...]
    select_n x1 -> x2, other arithmetic: 8.58 us -> 0.01 us  [the longest x1 0.01 us: experts(): shadow_rows = swap(by_source[hosts])]
    reduce_sum x5 -> x2, other arithmetic: 10.7 us -> 2.96 us  [the longest x1 1.65 us: attention(): jnp.sum(parts.reshape(kv_count, owners // kv_count, rows // owners, 2, wi...]
    ppermute x16 -> x6, starting transfers between devices: 21 us -> 16.5 us  [the longest x3 12.7 us: attention(): lax.ppermute(pair, 'ctx', [(c, c + step) for c in range(cycle - step)])]
  transfers between devices with their start and end apart: 21 -> 11, of which waited for: 10 -> 5; matrix products, arithmetic and copies ran while one was open for 12% -> 23% of each run, Pallas kernels for 0% -> 3%
where the time goes in v1:
time: 108 us; the launch traced here: 107 us
  starting transfers between devices  32 us (30%)
  waiting for transfers between devices  20.6 us (19%)
  matrix products  15.9 us (15%)
  between operations  14.3 us (13%)
  local copies, waits for them, and re-layouts  13.5 us (12%)
  other arithmetic  7.64 us (7%)
  Pallas kernels  2.99 us (3%)
    ppermute x3, starting transfers between devices, attention(): lax.ppermute(pair, 'ctx', [(c, c + step) for c in range(cycle - step)])  12.7 us
    dot_general x1, matrix products, experts(): lax.dot_general(weighted.reshape(owners * tokens, per_dev * units), gathe...  12.5 us
    ppermute x3, waiting for transfers between devices, attention(): lax.ppermute(terms[step], 'ctx', [(c, c - step) for c in range(step, cycl...  12 us
    all_to_all x1, waiting for transfers between devices, attention(): lax.all_to_all(total.astype(jnp.bfloat16), 'exp', split_axis=0, concat_ax...  5.64 us
    all_to_all x1, starting transfers between devices, experts(): by_source = swap(hidden[per_dev, :, :limit])  4.2 us
    all_to_all x1, starting transfers between devices, attention(): lax.all_to_all(total.astype(jnp.bfloat16), 'exp', split_axis=0, concat_ax...  4 us
    ppermute x3, starting transfers between devices, attention(): lax.ppermute(terms[step], 'ctx', [(c, c - step) for c in range(step, cycl...  3.88 us
    all_to_all x1, starting transfers between devices, experts(): probs = swap(table.T).reshape(owners, per_dev, tokens)  3.73 us
  transfers between devices with their start and end apart: 11, of which 5 were waited for; matrix products, arithmetic and copies ran while one was open for 23% of the time, Pallas kernels for 3%

profile of v1, /device:TPU:0, one launch (start us, length us, event | category | flops | bytes accessed | tf_op | source)
XLA Modules:
  0.0 106.9 jit_solution(14439129628927393718)
XLA Ops:
  7.2 0.0 all-gather.2.cloned.1.call-start
  7.2 0.7 all-gather.2.cloned.1.call-update
  8.0 0.9 constant_dynamic-slice_fusion
  8.8 0.7 fusion.30
  9.5 6.6 %collective-permute-start.1 = (bf16[256,256]{1,0:T(8,128)(2,1)}, bf16[256,256]{1,0:T(8,128)(2,1)}, u32[]{:S(2)}, u32[]{:S(2)}) collective-permute-start(bf16[256,256]{1,0:T(8,128)(2,1)} %get-tuple-element.14), channel_id=1, source_target_pairs={{0,16},{8,24},{1,17},{9,25},{2,18},{10,26},{3,19},{11,27},{4,20},{... | collective-permute-start | bytes 393224 | tf_op jit(solution)/shard_map/ppermute | solution.py:89
  16.1 4.1 %collective-permute-start = (bf16[256,256]{1,0:T(8,128)(2,1)}, bf16[256,256]{1,0:T(8,128)(2,1)}, u32[]{:S(2)}, u32[]{:S(2)}) collective-permute-start(bf16[256,256]{1,0:T(8,128)(2,1)} %get-tuple-element.14), channel_id=1, source_target_pairs={{0,8},{8,16},{16,24},{1,9},{9,17},{17,25},{2,10},{10,18},{18,26},{... | collective-permute-start | bytes 393224 | tf_op jit(solution)/shard_map/ppermute | solution.py:89
  20.2 1.9 %collective-permute-start.2 = (bf16[256,256]{1,0:T(8,128)(2,1)}, bf16[256,256]{1,0:T(8,128)(2,1)}, u32[]{:S(2)}, u32[]{:S(2)}) collective-permute-start(bf16[256,256]{1,0:T(8,128)(2,1)} %get-tuple-element.14), channel_id=1, source_target_pairs={{0,24},{1,25},{2,26},{3,27},{4,28},{5,29},{6,30},{7,31}} | collective-permute-start | bytes 393224 | tf_op jit(solution)/shard_map/ppermute | solution.py:89
  22.2 0.7 convert_element_type.78
  22.9 1.3 %select_reduce_fusion = bf16[128,16]{0,1:T(8,128)(2,1)} fusion(f32[128,8]{0,1:T(8,128)S(1)} %convert_element_type.78, s32[128,8]{0,1:T(8,128)} %param.19), kind=kLoop, calls=%fused_computation.39 | loop fusion | flops 47104 | bytes 12288 | tf_op jit(solution)/shard_map/reduce_sum | solution.py:152
  24.2 3.7 %all-to-all-start.1 = ((bf16[8,2,128]{2,1,0:T(2,128)(2,1)}), bf16[8,2,128]{2,1,0:T(2,128)(2,1)S(1)}, u32[]{:S(2)}, u32[]{:S(2)}) async-start(bf16[8,2,128]{2,1,0:T(2,128)(2,1)} %bitcast.12), calls=%async_computation.1 | async-start | bytes 8192 | tf_op jit(solution)/shard_map/all_to_all | solution.py:155
  27.9 0.7 reshape.87
  28.7 1.5 %copy.76 = bf16[1,3,8,65,384]{4,3,2,1,0:T(8,128)(2,1)S(1)} copy(bf16[1,3,8,65,384]{4,2,3,1,0:T(8,128)(2,1)} %param.23) | data formatting | bytes 2396160 | tf_op args[11]
  30.2 0.6 gather_fusion
  30.9 0.1 reduce_max.11
  31.0 0.6 pad_clamp_fusion
  31.6 0.8 slice_bitcast_fusion
  32.4 0.1 dynamic-slice_compare_fusion
  32.5 1.0 slice.35
  33.5 4.2 %all-to-all-start.2 = ((bf16[8,64,384]{2,1,0:T(8,128)(2,1)}), bf16[8,64,384]{2,1,0:T(8,128)(2,1)S(1)}, u32[]{:S(2)}, u32[]{:S(2)}) async-start(bf16[8,64,384]{2,1,0:T(8,128)(2,1)} %slice_bitcast_fusion), calls=%async_computation.2 | async-start | bytes 786432 | tf_op jit(solution)/shard_map/all_to_all | solution.py:158
  37.7 0.1 not_and_fusion
  37.8 0.1 convolution_convert_fusion.1
  38.0 1.1 %pad_maximum_fusion.pairs_ref = bf16[4,256,256]{2,1,0:T(8,128)(2,1)S(1)} fusion(bf16[1,256,256]{2,1,0:T(8,128)(2,1)} %bitcast.4, bf16[1,256,256]{2,1,0:T(8,128)(2,1)} %bitcast.3, bf16[1,256,256]{2,1,0:T(8,128)(2,1)} %bitcast.2, bf16[1,256,256]{2,1,0:T(8,128)(2,1)S(1)} %get-tuple-element.13), kind=kLoop, calls=%fused_computation.16 | loop fusion | flops 786432 | bytes 1048576 | tf_op jit(solution)/shard_map/stack | solution.py:106
  39.1 3.0 %attention.1 = (bf16[256,512]{1,0:T(8,128)(2,1)}, bf16[4,256,256]{2,1,0:T(8,128)(2,1)S(1)}) custom-call(s32[4]{0:T(128)S(1)} %compare_select_fusion.1.live_ref, bf16[256,512]{1,0:T(8,128)(2,1)S(1)} %copy-done.1, bf16[256,512]{1,0:T(8,128)(2,1)S(1)} %copy-done.2, bf16[256,512]{1,0:T(8,128)(2,1)S(1)} %copy-done.3, f32[4,256]{1,0:T(4,128)S(1)} %copy-done.4, ...), custom_call_target="tpu_custom_call" | custom-call | tf_op jit(solution)/shard_map/attention/pallas_call | solution.py:95
  42.1 1.3 %collective-permute-start.3 = (bf16[256,256]{1,0:T(8,128)(2,1)S(1)}, bf16[256,256]{1,0:T(8,128)(2,1)S(1)}, u32[]{:S(2)}, u32[]{:S(2)}) collective-permute-start(bf16[256,256]{1,0:T(8,128)(2,1)S(1)} %get-tuple-element.10), channel_id=1, source_target_pairs={{8,0},{16,8},{24,16},{9,1},{17,9},{25,17},{10,2},{18,10},{26,18},{... | collective-permute-start | bytes 393224 | tf_op jit(solution)/shard_map/ppermute | solution.py:109
  43.4 1.3 %collective-permute-start.5 = (bf16[256,256]{1,0:T(8,128)(2,1)S(1)}, bf16[256,256]{1,0:T(8,128)(2,1)S(1)}, u32[]{:S(2)}, u32[]{:S(2)}) collective-permute-start(bf16[256,256]{1,0:T(8,128)(2,1)S(1)} %get-tuple-element.11), channel_id=1, source_target_pairs={{24,0},{25,1},{26,2},{27,3},{28,4},{29,5},{30,6},{31,7}} | collective-permute-start | bytes 393224 | tf_op jit(solution)/shard_map/ppermute | solution.py:109
  44.7 1.3 %collective-permute-start.4 = (bf16[256,256]{1,0:T(8,128)(2,1)S(1)}, bf16[256,256]{1,0:T(8,128)(2,1)S(1)}, u32[]{:S(2)}, u32[]{:S(2)}) collective-permute-start(bf16[256,256]{1,0:T(8,128)(2,1)S(1)} %get-tuple-element.12), channel_id=1, source_target_pairs={{16,0},{24,8},{17,1},{25,9},{18,2},{26,10},{19,3},{27,11},{20,4},{... | collective-permute-start | bytes 393224 | tf_op jit(solution)/shard_map/ppermute | solution.py:109
  46.0 0.6 fusion.4
  46.7 3.3 %collective-permute-done.3 = bf16[256,256]{1,0:T(8,128)(2,1)S(1)} collective-permute-done((bf16[256,256]{1,0:T(8,128)(2,1)S(1)}, bf16[256,256]{1,0:T(8,128)(2,1)S(1)}, u32[]{:S(2)}, u32[]{:S(2)}) %collective-permute-start.3) | collective-permute-done | bytes 131104 | tf_op jit(solution)/shard_map/ppermute | solution.py:109
  49.9 3.6 %collective-permute-done.5 = bf16[256,256]{1,0:T(8,128)(2,1)S(1)} collective-permute-done((bf16[256,256]{1,0:T(8,128)(2,1)S(1)}, bf16[256,256]{1,0:T(8,128)(2,1)S(1)}, u32[]{:S(2)}, u32[]{:S(2)}) %collective-permute-start.5) | collective-permute-done | bytes 131104 | tf_op jit(solution)/shard_map/ppermute | solution.py:109
  53.5 5.1 %collective-permute-done.4 = bf16[256,256]{1,0:T(8,128)(2,1)S(1)} collective-permute-done((bf16[256,256]{1,0:T(8,128)(2,1)S(1)}, bf16[256,256]{1,0:T(8,128)(2,1)S(1)}, u32[]{:S(2)}, u32[]{:S(2)}) %collective-permute-start.4) | collective-permute-done | bytes 131104 | tf_op jit(solution)/shard_map/ppermute | solution.py:109
  58.6 0.7 fusion.14
  59.4 4.0 %all-to-all-start = ((bf16[8,32,256]{2,1,0:T(8,128)(2,1)}), bf16[8,32,256]{2,1,0:T(8,128)(2,1)}, u32[]{:S(2)}, u32[]{:S(2)}) async-start(bf16[8,32,256]{2,1,0:T(8,128)(2,1)} %bitcast.79), calls=%async_computation | async-start | bytes 262144 | tf_op jit(solution)/shard_map/all_to_all | solution.py:112
  63.4 0.1 convolution_convert_fusion
  63.5 1.5 %gather_fusion.1 = bf16[8,64,384]{2,1,0:T(8,128)(2,1)} fusion(bf16[8,64,384]{2,1,0:T(8,128)(2,1)S(1)} %all-to-all-done.2, s32[1024]{0:T(1024)} %pad_clamp_fusion), kind=kCustom, calls=%fused_computation.1 | custom fusion | bytes 786464 | tf_op jit(solution)/shard_map/gather | solution.py:160
  65.0 5.6 %all-to-all-done = bf16[8,32,256]{2,1,0:T(8,128)(2,1)} async-done(((bf16[8,32,256]{2,1,0:T(8,128)(2,1)}), bf16[8,32,256]{2,1,0:T(8,128)(2,1)}, u32[]{:S(2)}, u32[]{:S(2)}) %all-to-all-start) | async-done | bytes 131104 | tf_op jit(solution)/shard_map/all_to_all | solution.py:112
  70.6 3.5 %all-to-all-start.3 = ((bf16[8,64,384]{2,1,0:T(8,128)(2,1)}), bf16[8,64,384]{2,1,0:T(8,128)(2,1)S(1)}, u32[]{:S(2)}, u32[]{:S(2)}) async-start(bf16[8,64,384]{2,1,0:T(8,128)(2,1)} %gather_fusion.1), calls=%async_computation.3 | async-start | bytes 786432 | tf_op jit(solution)/shard_map/all_to_all | solution.py:160
  74.1 0.6 convert_bitcast_fusion
  74.7 1.6 %convert_element_type.74 = bf16[2,4,32,2,128]{4,3,2,1,0:T(2,128)(2,1)} reshape(bf16[8,32,256]{2,1,0:T(8,128)(2,1)} %all-to-all-done) | data formatting | bytes 262144 | tf_op jit(solution)/shard_map/convert_element_type | solution.py:116
  76.3 1.7 %reduce = bf16[2,32,2,128]{3,2,1,0:T(2,128)(2,1)} reduce(bf16[2,4,32,2,128]{4,3,2,1,0:T(2,128)(2,1)} %convert_element_type.74, bf16[]{:T(256)} %constant.58.clone.1), dimensions={1}, to_apply=%region_0.1.clone | reduce | flops 49152 | bytes 163842 | tf_op jit(solution)/shard_map/reduce_sum | solution.py:115
  78.0 0.9 fusion.31
  78.9 0.6 copy.77
  79.5 0.6 copy.78
  80.1 2.2 %all-to-all-done.3 = bf16[8,64,384]{2,1,0:T(8,128)(2,1)S(1)} async-done(((bf16[8,64,384]{2,1,0:T(8,128)(2,1)}), bf16[8,64,384]{2,1,0:T(8,128)(2,1)S(1)}, u32[]{:S(2)}, u32[]{:S(2)}) %all-to-all-start.3) | async-done | bytes 393248 | tf_op jit(solution)/shard_map/all_to_all | solution.py:160
  82.4 2.5 %fusion.3 = bf16[8,128,2,384]{3,1,2,0:T(8,128)(2,1)} fusion(f32[8,2,128,384]{3,2,1,0:T(8,128)S(1)} %fusion.4, f32[8,128,2]{1,2,0:T(2,128)} %convert_bitcast_fusion, bf16[8,64,384]{2,1,0:T(8,128)(2,1)S(1)} %all-to-all-done.3, s32[8,2,128]{2,1,0:T(2,128)S(1)} %copy.56, pred[8,2,128]{2,1,0:T(4,128)(4,1)} %copy-done.7), kind=kOutput, calls=%fused_computation.6 | convolution fusion | flops 103546880 | bytes 5130240 | tf_op jit(solution)/shard_map/sjtr,srf->stjf/dot_general | solution.py:170
  84.9 2.2 %copy.58 = bf16[8,128,2,384]{1,0,3,2:T(8,128)(2,1)S(1)} copy(bf16[8,128,2,384]{3,1,2,0:T(8,128)(2,1)} %fusion.3) | data formatting | bytes 3145728 | tf_op jit(solution)/shard_map/convert_element_type | solution.py:172
  87.0 0.4 copy.75
  87.5 0.0 all-gather.2.cloned.1.call-done
  87.5 12.5 %fusion = f32[2,384,4096]{2,1,0:T(8,128)} fusion(bf16[2,384,1024]{2,1,0:T(8,128)(2,1)S(1)} %bitcast.78, bf16[1024,4096]{1,0:T(8,128)(2,1)} %all-gather.2.cloned.1.call-done), kind=kOutput, calls=%fused_computation.2 | convolution fusion | flops 6442450944 | bytes 22544384 | tf_op jit(solution)/shard_map/dot_general | solution.py:173
  (32 shorter events, 0.2 us)
Async XLA Ops:
  7.2 23.0 %copy-start = (s32[4,4]{1,0:T(4,128)S(1)}, s32[4,4]{1,0:T(4,128)}, u32[]{:S(2)}) copy-start(s32[4,4]{1,0:T(4,128)} %param.18) | copy-start | bytes 196
  7.2 25.3 %copy-start.8 = (s32[16]{0:T(128)S(1)}, s32[16]{0:T(128)}, u32[]{:S(2)}) copy-start(s32[16]{0:T(128)} %param.22) | copy-start | bytes 196
  7.2 25.3 %copy-start.6 = (bf16[1,3,8,65,384]{4,2,3,1,0:T(8,128)(2,1)S(1)}, bf16[1,3,8,65,384]{4,2,3,1,0:T(8,128)(2,1)}, u32[]{:S(2)}) copy-start(bf16[1,3,8,65,384]{4,2,3,1,0:T(8,128)(2,1)} %param.23) | copy-start | bytes 3594244
  7.2 80.3 %all-gather.2.cloned.1.call-start = ((), (), s32[]{:S(2)}) async-start(), calls=%async_computation.4 | async-start | bytes 9437184 | tf_op jit(solution)/shard_map/all_gather | solution.py:149
  9.5 28.4 %collective-permute-start.1 = (bf16[256,256]{1,0:T(8,128)(2,1)}, bf16[256,256]{1,0:T(8,128)(2,1)}, u32[]{:S(2)}, u32[]{:S(2)}) collective-permute-start(bf16[256,256]{1,0:T(8,128)(2,1)} %get-tuple-element.14), channel_id=1, source_target_pairs={{0,16},{8,24},{1,17},{9,25},{2,18},{10,26},{3,19},{11,27},{4,20},{... | collective-permute-start | bytes 393224 | tf_op jit(solution)/shard_map/ppermute | solution.py:89
  16.1 21.8 %collective-permute-start = (bf16[256,256]{1,0:T(8,128)(2,1)}, bf16[256,256]{1,0:T(8,128)(2,1)}, u32[]{:S(2)}, u32[]{:S(2)}) collective-permute-start(bf16[256,256]{1,0:T(8,128)(2,1)} %get-tuple-element.14), channel_id=1, source_target_pairs={{0,8},{8,16},{16,24},{1,9},{9,17},{17,25},{2,10},{10,18},{18,26},{... | collective-permute-start | bytes 393224 | tf_op jit(solution)/shard_map/ppermute | solution.py:89
  20.2 17.7 %collective-permute-start.2 = (bf16[256,256]{1,0:T(8,128)(2,1)}, bf16[256,256]{1,0:T(8,128)(2,1)}, u32[]{:S(2)}, u32[]{:S(2)}) collective-permute-start(bf16[256,256]{1,0:T(8,128)(2,1)} %get-tuple-element.14), channel_id=1, source_target_pairs={{0,24},{1,25},{2,26},{3,27},{4,28},{5,29},{6,30},{7,31}} | collective-permute-start | bytes 393224 | tf_op jit(solution)/shard_map/ppermute | solution.py:89
  24.2 9.3 %all-to-all-start.1 = ((bf16[8,2,128]{2,1,0:T(2,128)(2,1)}), bf16[8,2,128]{2,1,0:T(2,128)(2,1)S(1)}, u32[]{:S(2)}, u32[]{:S(2)}) async-start(bf16[8,2,128]{2,1,0:T(2,128)(2,1)} %bitcast.12), calls=%async_computation.1 | async-start | bytes 8192 | tf_op jit(solution)/shard_map/all_to_all | solution.py:155
  28.6 10.4 %copy-start.1 = (bf16[256,512]{1,0:T(8,128)(2,1)S(1)}, bf16[256,512]{1,0:T(8,128)(2,1)}, u32[]{:S(2)}) copy-start(bf16[256,512]{1,0:T(8,128)(2,1)} %query_ref.1) | copy-start | bytes 786436
  28.6 10.4 %copy-start.2 = (bf16[256,512]{1,0:T(8,128)(2,1)S(1)}, bf16[256,512]{1,0:T(8,128)(2,1)}, u32[]{:S(2)}) copy-start(bf16[256,512]{1,0:T(8,128)(2,1)} %grad_ref.1) | copy-start | bytes 786436
  28.6 10.4 %copy-start.3 = (bf16[256,512]{1,0:T(8,128)(2,1)S(1)}, bf16[256,512]{1,0:T(8,128)(2,1)}, u32[]{:S(2)}) copy-start(bf16[256,512]{1,0:T(8,128)(2,1)} %out_ref.1) | copy-start | bytes 786436
  28.6 10.4 %copy-start.4 = (f32[4,256]{1,0:T(4,128)S(1)}, f32[4,256]{1,0:T(4,128)}, u32[]{:S(2)}) copy-start(f32[4,256]{1,0:T(4,128)} %lse_ref.1) | copy-start | bytes 12292
  33.5 25.9 %all-to-all-start.2 = ((bf16[8,64,384]{2,1,0:T(8,128)(2,1)}), bf16[8,64,384]{2,1,0:T(8,128)(2,1)S(1)}, u32[]{:S(2)}, u32[]{:S(2)}) async-start(bf16[8,64,384]{2,1,0:T(8,128)(2,1)} %slice_bitcast_fusion), calls=%async_computation.2 | async-start | bytes 786432 | tf_op jit(solution)/shard_map/all_to_all | solution.py:158
  37.7 8.3 %copy-start.5 = (bf16[1,2,8,65,384]{4,2,3,1,0:T(8,128)(2,1)S(1)}, bf16[1,2,8,65,384]{4,2,3,1,0:T(8,128)(2,1)}, u32[]{:S(2)}) copy-start(bf16[1,2,8,65,384]{4,2,3,1,0:T(8,128)(2,1)} %slice.35) | copy-start | bytes 2396164
  37.8 25.6 %copy-start.7 = (pred[8,2,128]{2,1,0:T(4,128)(4,1)}, pred[8,2,128]{2,1,0:T(4,128)(4,1)S(1)}, u32[]{:S(2)}) copy-start(pred[8,2,128]{2,1,0:T(4,128)(4,1)S(1)} %get-tuple-element.9) | copy-start | bytes 6148
  42.1 7.8 %collective-permute-start.3 = (bf16[256,256]{1,0:T(8,128)(2,1)S(1)}, bf16[256,256]{1,0:T(8,128)(2,1)S(1)}, u32[]{:S(2)}, u32[]{:S(2)}) collective-permute-start(bf16[256,256]{1,0:T(8,128)(2,1)S(1)} %get-tuple-element.10), channel_id=1, source_target_pairs={{8,0},{16,8},{24,16},{9,1},{17,9},{25,17},{10,2},{18,10},{26,18},{... | collective-permute-start | bytes 393224 | tf_op jit(solution)/shard_map/ppermute | solution.py:109
  43.4 10.1 %collective-permute-start.5 = (bf16[256,256]{1,0:T(8,128)(2,1)S(1)}, bf16[256,256]{1,0:T(8,128)(2,1)S(1)}, u32[]{:S(2)}, u32[]{:S(2)}) collective-permute-start(bf16[256,256]{1,0:T(8,128)(2,1)S(1)} %get-tuple-element.11), channel_id=1, source_target_pairs={{24,0},{25,1},{26,2},{27,3},{28,4},{29,5},{30,6},{31,7}} | collective-permute-start | bytes 393224 | tf_op jit(solution)/shard_map/ppermute | solution.py:109
  44.7 13.9 %collective-permute-start.4 = (bf16[256,256]{1,0:T(8,128)(2,1)S(1)}, bf16[256,256]{1,0:T(8,128)(2,1)S(1)}, u32[]{:S(2)}, u32[]{:S(2)}) collective-permute-start(bf16[256,256]{1,0:T(8,128)(2,1)S(1)} %get-tuple-element.12), channel_id=1, source_target_pairs={{16,0},{24,8},{17,1},{25,9},{18,2},{26,10},{19,3},{27,11},{20,4},{... | collective-permute-start | bytes 393224 | tf_op jit(solution)/shard_map/ppermute | solution.py:109
  59.4 11.3 %all-to-all-start = ((bf16[8,32,256]{2,1,0:T(8,128)(2,1)}), bf16[8,32,256]{2,1,0:T(8,128)(2,1)}, u32[]{:S(2)}, u32[]{:S(2)}) async-start(bf16[8,32,256]{2,1,0:T(8,128)(2,1)} %bitcast.79), calls=%async_computation | async-start | bytes 262144 | tf_op jit(solution)/shard_map/all_to_all | solution.py:112
  70.6 11.7 %all-to-all-start.3 = ((bf16[8,64,384]{2,1,0:T(8,128)(2,1)}), bf16[8,64,384]{2,1,0:T(8,128)(2,1)S(1)}, u32[]{:S(2)}, u32[]{:S(2)}) async-start(bf16[8,64,384]{2,1,0:T(8,128)(2,1)} %gather_fusion.1), calls=%async_computation.3 | async-start | bytes 786432 | tf_op jit(solution)/shard_map/all_to_all | solution.py:160
Sparse Core Ops, SparseCore 0:
  9.9 61.6 all-gather.1

commit v2 on v1

--- a/solution.py
+++ b/solution.py
@@ -121,62 +121,146 @@
     return (query_grad, final[0], final[1])
 
 
-def rows_of_pairs(named, capacity):
-    tokens = named.shape[-1]
-    ones = named.astype(jnp.bfloat16)
-    before = (
+def weight_kernel(order_ref, flag_ref, probs_ref, hidden_ref, shadow_ref, weight_ref):
+    per_dev, tokens = probs_ref.shape[1:]
+    units = hidden_ref.shape[4]
+    earlier = (
         lax.broadcasted_iota(jnp.int32, (tokens, tokens), 0)
         < lax.broadcasted_iota(jnp.int32, (tokens, tokens), 1)
     ).astype(jnp.bfloat16)
-    rank = jnp.einsum("...u,ut->...t", ones, before, preferred_element_type=jnp.float32)
-    place = jnp.arange(capacity, dtype=jnp.int32)
-    return jnp.where(
-        named[..., None] & (rank.astype(jnp.int32)[..., None] == place), 1.0, 0.0
-    ).astype(jnp.bfloat16)
+    odd = lax.broadcasted_iota(jnp.int32, (1, tokens), 1) % 2 == 1
+
+    def rows_at(named, rows):
+        rank = jnp.dot(
+            jnp.broadcast_to(named.astype(jnp.float32), (8, tokens)).astype(jnp.bfloat16),
+            earlier,
+            preferred_element_type=jnp.float32,
+        )[:1]
+        place = lax.broadcasted_iota(jnp.int32, (rows.shape[0], tokens), 0).astype(jnp.float32)
+        chosen = jnp.where(jnp.logical_and(named, rank == place), 1.0, 0.0).astype(jnp.bfloat16)
+        return lax.dot_general(rows, chosen, FIRST, preferred_element_type=jnp.float32)
+
+    for j in range(per_dev):
+        prob = probs_ref[0, j : j + 1].astype(jnp.float32)
+        named = prob > 0
+        side = jnp.logical_and(jnp.logical_and(named, odd), flag_ref[j] > 0)
+        own = jnp.logical_and(named, jnp.logical_not(side))
+        rows = rows_at(own, hidden_ref[0, j, 0]) + rows_at(side, shadow_ref[0])
+        weight_ref[j * units : (j + 1) * units] = (rows * prob).astype(jnp.bfloat16)
+
+
+def weighted_rows(probs, hidden, shadow_rows, flags, order):
+    owners, per_dev, tokens = probs.shape
+    units = hidden.shape[4]
+    return pl.pallas_call(
+        weight_kernel,
+        out_shape=jax.ShapeDtypeStruct((per_dev * units, owners * tokens), jnp.bfloat16),
+        grid_spec=pltpu.PrefetchScalarGridSpec(
+            num_scalar_prefetch=2,
+            grid=(owners,),
+            in_specs=[
+                pl.BlockSpec((1, per_dev, tokens), lambda i, order, flag: (order[i], 0, 0)),
+                pl.BlockSpec(
+                    (1, per_dev, 1) + hidden.shape[3:],
+                    lambda i, order, flag: (0, 0, order[i], 0, 0),
+                ),
+                pl.BlockSpec(
+                    (1,) + shadow_rows.shape[1:], lambda i, order, flag: (order[i], 0, 0)
+                ),
+            ],
+            out_specs=pl.BlockSpec((per_dev * units, tokens), lambda i, order, flag: (0, i)),
+        ),
+        compiler_params=pltpu.CompilerParams(vmem_limit_bytes=40 * 2**20),
+        name="weighted",
+    )(order, flags, probs, hidden, shadow_rows)
+
+
+def tile_kernel(weight_ref, first_ref, second_ref, *rest):
+    tile_ref = rest[-1]
+    depth = first_ref.shape[0]
+    tile_ref[...] = jnp.dot(
+        weight_ref[:, :depth], first_ref[...], preferred_element_type=jnp.float32
+    ) + jnp.dot(weight_ref[:, depth:], second_ref[...], preferred_element_type=jnp.float32)
+
+
+def tile_columns(weighted, first, second, width, start, tiles):
+    depth, columns = first.shape
+    rows = weighted.shape[0]
+    step = min(512, columns)
+    shift = start // step
+    gathered = pl.BlockSpec((depth, step), lambda i: (0, i))
+    earlier = [] if tiles is None else [tiles]
+    return pl.pallas_call(
+        tile_kernel,
+        out_shape=jax.ShapeDtypeStruct((rows, width), jnp.float32),
+        grid=(columns // step,),
+        in_specs=[pl.BlockSpec(weighted.shape, lambda i: (0, 0)), gathered, gathered]
+        + [pl.BlockSpec(memory_space=pl.ANY)] * len(earlier),
+        out_specs=pl.BlockSpec((rows, step), lambda i: (0, i + shift)),
+        input_output_aliases={3: 0} if earlier else {},
+        compiler_params=pltpu.CompilerParams(vmem_limit_bytes=40 * 2**20),
+        name="tiles",
+    )(weighted, first, second, *earlier)
 
 
 def experts(expert_ids, route_probs, moe_grad, shadow_list, stored_hidden_state):
     owners = lax.axis_size("exp")
     own_index = lax.axis_index("exp")
-    tokens = expert_ids.shape[0]
+    tokens, model = moe_grad.shape
     count = shadow_list.shape[0]
     per_dev = count // owners
-    hidden = stored_hidden_state[0]
-    units = hidden.shape[-1]
+    units = stored_hidden_state.shape[4]
+    chips = owners // 2
+    alike = [[2 * chip + core for chip in range(chips)] for core in range(2)]
     swap = functools.partial(
         lax.all_to_all, axis_name="exp", split_axis=0, concat_axis=0, tiled=True
     )
-    gathered = lax.all_gather(moe_grad, "exp", tiled=True)
+    parts = 2
+    gathered = [
+        lax.all_gather(columns, "exp", axis_index_groups=alike, tiled=True)
+        for columns in jnp.split(moe_grad, parts, axis=1)
+    ]
 
     hit = expert_ids[:, None, :] == jnp.arange(count, dtype=jnp.int32)[None, :, None]
     table = jnp.sum(
         jnp.where(hit, route_probs[:, None, :].astype(jnp.float32), 0.0), axis=2
     ).astype(jnp.bfloat16)
-    probs = swap(table.T).reshape(owners, per_dev, tokens)
-
-    limit = min(hidden.shape[2], tokens // 2)
-    by_source = swap(hidden[per_dev, :, :limit])
+    table = table.T.reshape(owners, per_dev * tokens)
+    extra = -(-table.shape[1] // units)
+    table = jnp.pad(table, ((0, 0), (0, extra * units - table.shape[1])))
+    limit = min(stored_hidden_state.shape[3], tokens // 2)
+    mixed = swap(
+        jnp.concatenate(
+            [stored_hidden_state[0, per_dev, :, :limit], table.reshape(owners, extra, units)],
+            axis=1,
+        )
+    )
+    probs = mixed[:, limit:].reshape(owners, extra * units)[:, : per_dev * tokens]
+    probs = probs.reshape(owners, per_dev, tokens)
     hosts = jnp.max(shadow_list.reshape(owners, per_dev), axis=1)
-    shadow_rows = swap(by_source[hosts])
-
+    shadow_rows = swap(mixed[:, :limit][hosts])
     flags = lax.dynamic_slice_in_dim(shadow_list, own_index * per_dev, per_dev) >= 0
-    odd = jnp.arange(tokens, dtype=jnp.int32) % 2 == 1
-    named = probs > 0
-    side = named & odd & flags[None, :, None]
-    own_place = rows_of_pairs(named & ~side, hidden.shape[2])
-    side_place = rows_of_pairs(side, limit)
-    rows = jnp.einsum(
-        "sjtr,jsrf->stjf", own_place, hidden[:per_dev], preferred_element_type=jnp.float32
-    ) + jnp.einsum("sjtr,srf->stjf", side_place, shadow_rows, preferred_element_type=jnp.float32)
-    weight = jnp.transpose(probs, (0, 2, 1))[..., None].astype(jnp.float32)
-    weighted = (rows * weight).astype(jnp.bfloat16)
-    tiles = lax.dot_general(
-        weighted.reshape(owners * tokens, per_dev * units),
-        gathered,
-        FIRST,
-        preferred_element_type=jnp.float32,
-    )
-    return tiles.reshape(per_dev, units, moe_grad.shape[1])
+    place = jnp.arange(owners, dtype=jnp.int32)
+    order = 2 * (place % chips) + (place // chips + own_index) % 2
+    weighted = weighted_rows(
+        probs, stored_hidden_state, shadow_rows, flags.astype(jnp.int32), order
+    )
+    return weighted, gathered
+
+
+def expert_tiles(weighted, gathered, anchors, per_dev):
+    owners = lax.axis_size("exp")
+    model = sum(first.shape[1] for first in gathered)
+    pairs, second = [], None
+    for first, anchor in zip(gathered, anchors):
+        first, _ = lax.optimization_barrier((first, (anchor, second)))
+        second = lax.ppermute(first, "exp", [(e, e ^ 1) for e in range(owners)])
+        pairs.append((first, second))
+    tiles, start = None, 0
+    for first, second in pairs:
+        tiles = tile_columns(weighted, first, second, model, start, tiles)
+        start += first.shape[1]
+    return tiles.reshape(per_dev, weighted.shape[0] // per_dev, model)
 
 
 def local(
@@ -196,7 +280,11 @@
     query_grad, key_grad, value_grad = attention(
         queries, keys, values, attn_out, attn_out_grad, lse_excess, block_mask
     )
-    expert_grad = experts(expert_ids, route_probs, moe_grad, shadow_list, stored_hidden_state)
+    weighted, gathered = experts(
+        expert_ids, route_probs, moe_grad, shadow_list, stored_hidden_state
+    )
+    per_dev = shadow_list.shape[0] // lax.axis_size("exp")
+    expert_grad = expert_tiles(weighted, gathered, (weighted, (key_grad, value_grad)), per_dev)
     return (query_grad, key_grad, value_grad, expert_grad)
 
 

time: 108 us -> 124 us (1.15)
  waiting for transfers between devices: 20.6 us -> 45.4 us
  Pallas kernels: 2.99 us -> 19.8 us
  matrix products: 15.9 us -> 0 us
  starting transfers between devices: 32 us -> 22.3 us
  blocking collectives: 0 us -> 8.07 us
  other arithmetic: 7.64 us -> 1.42 us
  local copies, waits for them, and re-layouts: 13.5 us -> 11.5 us
    pallas_call x0 -> x3, Pallas kernels: none -> 16.8 us  [the longest x2 12.5 us: tile_columns(): pl.pallas_call(tile_kernel, out_shape=jax.ShapeDtypeStruct((rows, width),...]
    dot_general x5 -> x0, matrix products: 15.9 us -> none  [the longest x1 12.5 us: experts(): lax.dot_general(weighted.reshape(owners * tokens, per_dev * units), gathe...]
    all_to_all x4 -> x2, waiting for transfers between devices: 7.88 us -> 20.1 us  [the longest x1 10.3 us: experts(): swap(jnp.concatenate([stored_hidden_state[0, per_dev, :, :limit], table.r...]
    all_to_all x0 -> x1, blocking collectives: none -> 8.07 us  [attention(): lax.all_to_all(total.astype(jnp.bfloat16), 'exp', split_axis=0, concat_ax...]
    all_to_all x4 -> x2, starting transfers between devices: 15.4 us -> 8.75 us  [the longest x1 5.17 us: experts(): swap(jnp.concatenate([stored_hidden_state[0, per_dev, :, :limit], table.r...]
    all_gather x1 -> x2, waiting for transfers between devices: 0.02 us -> 4.63 us  [experts(): lax.all_gather(columns, 'exp', axis_index_groups=alike, tiled=True)]
    ppermute x3, waiting for transfers between devices: 12 us -> 15.9 us  [attention(): lax.ppermute(terms[step], 'ctx', [(c, c - step) for c in range(step, cycl...]
    ppermute x3, waiting for transfers between devices: 0.01 us -> 3.93 us  [attention(): lax.ppermute(pair, 'ctx', [(c, c + step) for c in range(cycle - step)])]
  transfers between devices with their start and end apart: 11 -> 12, of which waited for: 5 -> 8; matrix products, arithmetic and copies ran while one was open for 23% -> 5% of each run, Pallas kernels for 3% -> 12%
where the time goes in v2:
time: 124 us; the launch traced here: 123 us
  waiting for transfers between devices  45.4 us (37%)
  starting transfers between devices  22.3 us (18%)
  Pallas kernels  19.8 us (16%)
  between operations  14.4 us (12%)
  local copies, waits for them, and re-layouts  11.5 us (9%)
  blocking collectives  8.07 us (7%)
  other arithmetic  1.42 us (1%)
    ppermute x3, waiting for transfers between devices, attention(): lax.ppermute(terms[step], 'ctx', [(c, c - step) for c in range(step, cycl...  15.9 us
    pallas_call x2, Pallas kernels, tile_columns(): pl.pallas_call(tile_kernel, out_shape=jax.ShapeDtypeStruct((rows, width),...  12.5 us
    all_to_all x1, waiting for transfers between devices, experts(): swap(jnp.concatenate([stored_hidden_state[0, per_dev, :, :limit], table.r...  10.3 us
    all_to_all x1, waiting for transfers between devices, experts(): shadow_rows = swap(mixed[:, :limit][hosts])  9.82 us
    ppermute x3, starting transfers between devices, attention(): lax.ppermute(pair, 'ctx', [(c, c + step) for c in range(cycle - step)])  9.58 us
    all_to_all x1, blocking collectives, attention(): lax.all_to_all(total.astype(jnp.bfloat16), 'exp', split_axis=0, concat_ax...  8.07 us
    unnamed x28, local copies, waits for them, and re-layouts  5.87 us
    all_to_all x1, starting transfers between devices, experts(): swap(jnp.concatenate([stored_hidden_state[0, per_dev, :, :limit], table.r...  5.17 us
  transfers between devices with their start and end apart: 12, of which 8 were waited for; matrix products, arithmetic and copies ran while one was open for 5% of the time, Pallas kernels for 12%

profile of v2, /device:TPU:0, one launch (start us, length us, event | category | flops | bytes accessed | tf_op | source)
XLA Modules:
  0.0 122.8 jit_solution(3822962722167109616)
XLA Ops:
  7.2 0.0 copy-start
  7.2 0.0 all-gather.5.cloned.1.call-start
  7.3 2.4 %fusion.9 = (bf16[128,2048]{1,0:T(8,128)(2,1)}, bf16[128,2048]{1,0:T(8,128)(2,1)}) fusion(bf16[128,4096]{1,0:T(8,128)(2,1)} %param.21), kind=kLoop, calls=%fused_computation.40 | loop fusion | bytes 2097152 | tf_op jit(solution)/shard_map/split | solution.py:221
  9.6 0.0 all-gather.5.cloned.1.call-update
  9.7 0.0 all-gather.3.cloned.1.call-start
  9.7 0.7 all-gather.3.cloned.1.call-update
  10.5 0.0 copy-start.11
  10.5 0.2 copy.43.hidden_ref
  10.8 0.8 pad_maximum_fusion.1
  11.6 5.2 %all-to-all-start.1 = ((bf16[8,65,384]{2,1,0:T(8,128)(2,1)}), bf16[8,65,384]{2,1,0:T(8,128)(2,1)S(1)}, u32[]{:S(2)}, u32[]{:S(2)}) async-start(bf16[8,65,384]{2,1,0:T(8,128)(2,1)} %pad_maximum_fusion.1), calls=%async_computation.1 | async-start | bytes 884736 | tf_op jit(solution)/shard_map/all_to_all | solution.py:232
  16.8 0.1 reshape.70
  16.9 0.1 reduce_max.11
  17.0 10.3 %all-to-all-done.1 = bf16[8,65,384]{2,1,0:T(8,128)(2,1)S(1)} async-done(((bf16[8,65,384]{2,1,0:T(8,128)(2,1)}), bf16[8,65,384]{2,1,0:T(8,128)(2,1)S(1)}, u32[]{:S(2)}, u32[]{:S(2)}) %all-to-all-start.1) | async-done | bytes 399392 | tf_op jit(solution)/shard_map/all_to_all | solution.py:232
  27.4 1.3 %gather_fusion.1 = bf16[8,64,384]{2,1,0:T(8,128)(2,1)} fusion(bf16[8,64,384]{2,1,0:T(8,128)(2,1)S(1)} %slice.51, s32[1024]{0:T(1024)S(1)} %pad_clamp_fusion), kind=kCustom, calls=%fused_computation.1 | custom fusion | bytes 786464 | tf_op jit(solution)/shard_map/gather | solution.py:241
  28.7 3.6 %all-to-all-start.2 = ((bf16[8,64,384]{2,1,0:T(8,128)(2,1)}), bf16[8,64,384]{2,1,0:T(8,128)(2,1)S(1)}, u32[]{:S(2)}, u32[]{:S(2)}) async-start(bf16[8,64,384]{2,1,0:T(8,128)(2,1)} %gather_fusion.1), calls=%async_computation.2 | async-start | bytes 786432 | tf_op jit(solution)/shard_map/all_to_all | solution.py:241
  32.4 0.1 compare_convert_fusion.flag_ref
  32.5 0.0 copy-start.6
  32.5 9.8 %all-to-all-done.2.shadow_ref = bf16[8,64,384]{2,1,0:T(8,128)(2,1)S(1)} async-done(((bf16[8,64,384]{2,1,0:T(8,128)(2,1)}), bf16[8,64,384]{2,1,0:T(8,128)(2,1)S(1)}, u32[]{:S(2)}, u32[]{:S(2)}) %all-to-all-start.2) | async-done | bytes 393248 | tf_op jit(solution)/shard_map/all_to_all | solution.py:241
  42.3 4.3 %weighted.1.weight_ref = bf16[768,1024]{1,0:T(8,128)(2,1)S(1)} custom-call(s32[8]{0:T(128)S(1)} %fusion.3.order_ref, s32[2]{0:T(128)S(1)} %compare_convert_fusion.flag_ref, bf16[8,2,128]{2,1,0:T(2,128)(2,1)S(1)} %reshape.69.probs_ref, bf16[1,3,8,65,384]{4,3,2,1,0:T(8,128)(2,1)S(1)} %copy.43.hidden_ref, bf16[8,64,384]{2,1,0:T(8,128)(2,1)S(1)} %all-to-all-done.2.shadow_ref), custom_call_target="tpu_custom_call" | custom-call | tf_op jit(solution)/shard_map/weighted/pallas_call | solution.py:155
  46.6 4.6 %all-gather.5.cloned.1.call-done.first_ref = bf16[512,2048]{1,0:T(8,128)(2,1)} async-done(((bf16[128,2048]{1,0:T(8,128)(2,1)}), bf16[512,2048]{1,0:T(8,128)(2,1)}) %all-gather.5.cloned.1.call-update) | async-done | bytes 2097168 | tf_op jit(solution)/shard_map/all_gather | solution.py:220
  51.3 0.0 collective-permute-start.6
  51.3 0.9 constant_dynamic-slice_fusion
  52.2 4.7 %collective-permute-start.1 = (bf16[256,256]{1,0:T(8,128)(2,1)S(1)}, bf16[256,256]{1,0:T(8,128)(2,1)S(1)}, u32[]{:S(2)}, u32[]{:S(2)}) collective-permute-start(bf16[256,256]{1,0:T(8,128)(2,1)S(1)} %get-tuple-element.18), channel_id=1, source_target_pairs={{0,16},{8,24},{1,17},{9,25},{2,18},{10,26},{3,19},{11,27},{4,20},{... | collective-permute-start | bytes 393224 | tf_op jit(solution)/shard_map/ppermute | solution.py:89
  56.9 3.6 %collective-permute-start = (bf16[256,256]{1,0:T(8,128)(2,1)S(1)}, bf16[256,256]{1,0:T(8,128)(2,1)S(1)}, u32[]{:S(2)}, u32[]{:S(2)}) collective-permute-start(bf16[256,256]{1,0:T(8,128)(2,1)S(1)} %get-tuple-element.18), channel_id=1, source_target_pairs={{0,8},{8,16},{16,24},{1,9},{9,17},{17,25},{2,10},{10,18},{18,26},{... | collective-permute-start | bytes 393224 | tf_op jit(solution)/shard_map/ppermute | solution.py:89
  60.5 1.3 %collective-permute-start.2 = (bf16[256,256]{1,0:T(8,128)(2,1)S(1)}, bf16[256,256]{1,0:T(8,128)(2,1)S(1)}, u32[]{:S(2)}, u32[]{:S(2)}) collective-permute-start(bf16[256,256]{1,0:T(8,128)(2,1)S(1)} %get-tuple-element.18), channel_id=1, source_target_pairs={{0,24},{1,25},{2,26},{3,27},{4,28},{5,29},{6,30},{7,31}} | collective-permute-start | bytes 393224 | tf_op jit(solution)/shard_map/ppermute | solution.py:89
  61.8 0.6 gather_fusion
  62.5 1.8 %collective-permute-done = bf16[256,256]{1,0:T(8,128)(2,1)S(1)} collective-permute-done((bf16[256,256]{1,0:T(8,128)(2,1)S(1)}, bf16[256,256]{1,0:T(8,128)(2,1)S(1)}, u32[]{:S(2)}, u32[]{:S(2)}) %collective-permute-start) | collective-permute-done | bytes 131104 | tf_op jit(solution)/shard_map/ppermute | solution.py:89
  64.3 2.1 %collective-permute-done.2 = bf16[256,256]{1,0:T(8,128)(2,1)S(1)} collective-permute-done((bf16[256,256]{1,0:T(8,128)(2,1)S(1)}, bf16[256,256]{1,0:T(8,128)(2,1)S(1)}, u32[]{:S(2)}, u32[]{:S(2)}) %collective-permute-start.2) | collective-permute-done | bytes 131104 | tf_op jit(solution)/shard_map/ppermute | solution.py:89
  66.4 0.1 pad_maximum_fusion.pairs_ref
  66.5 0.0 copy-start.3
  66.5 0.9 copy-done.3
  67.4 0.9 copy-done.4
  68.4 0.9 copy-done.5
  69.3 3.0 %attention.1 = (bf16[256,512]{1,0:T(8,128)(2,1)}, bf16[4,256,256]{2,1,0:T(8,128)(2,1)S(1)}) custom-call(s32[4]{0:T(128)S(1)} %compare_select_fusion.3.live_ref, bf16[256,512]{1,0:T(8,128)(2,1)S(1)} %copy-done.3, bf16[256,512]{1,0:T(8,128)(2,1)S(1)} %copy-done.4, bf16[256,512]{1,0:T(8,128)(2,1)S(1)} %copy-done.5, f32[4,256]{1,0:T(4,128)S(1)} %copy-done.6, ...), custom_call_target="tpu_custom_call" | custom-call | tf_op jit(solution)/shard_map/attention/pallas_call | solution.py:95
  72.4 1.3 %collective-permute-start.3 = (bf16[256,256]{1,0:T(8,128)(2,1)S(1)}, bf16[256,256]{1,0:T(8,128)(2,1)S(1)}, u32[]{:S(2)}, u32[]{:S(2)}) collective-permute-start(bf16[256,256]{1,0:T(8,128)(2,1)S(1)} %get-tuple-element.14), channel_id=1, source_target_pairs={{8,0},{16,8},{24,16},{9,1},{17,9},{25,17},{10,2},{18,10},{26,18},{... | collective-permute-start | bytes 393224 | tf_op jit(solution)/shard_map/ppermute | solution.py:109
  73.7 1.3 %collective-permute-start.5 = (bf16[256,256]{1,0:T(8,128)(2,1)S(1)}, bf16[256,256]{1,0:T(8,128)(2,1)S(1)}, u32[]{:S(2)}, u32[]{:S(2)}) collective-permute-start(bf16[256,256]{1,0:T(8,128)(2,1)S(1)} %get-tuple-element.15), channel_id=1, source_target_pairs={{24,0},{25,1},{26,2},{27,3},{28,4},{29,5},{30,6},{31,7}} | collective-permute-start | bytes 393224 | tf_op jit(solution)/shard_map/ppermute | solution.py:109
  75.0 1.3 %collective-permute-start.4 = (bf16[256,256]{1,0:T(8,128)(2,1)S(1)}, bf16[256,256]{1,0:T(8,128)(2,1)S(1)}, u32[]{:S(2)}, u32[]{:S(2)}) collective-permute-start(bf16[256,256]{1,0:T(8,128)(2,1)S(1)} %get-tuple-element.16), channel_id=1, source_target_pairs={{16,0},{24,8},{17,1},{25,9},{18,2},{26,10},{19,3},{27,11},{20,4},{... | collective-permute-start | bytes 393224 | tf_op jit(solution)/shard_map/ppermute | solution.py:109
  76.3 5.5 %collective-permute-done.3 = bf16[256,256]{1,0:T(8,128)(2,1)S(1)} collective-permute-done((bf16[256,256]{1,0:T(8,128)(2,1)S(1)}, bf16[256,256]{1,0:T(8,128)(2,1)S(1)}, u32[]{:S(2)}, u32[]{:S(2)}) %collective-permute-start.3) | collective-permute-done | bytes 131104 | tf_op jit(solution)/shard_map/ppermute | solution.py:109
  81.8 6.9 %collective-permute-done.5 = bf16[256,256]{1,0:T(8,128)(2,1)S(1)} collective-permute-done((bf16[256,256]{1,0:T(8,128)(2,1)S(1)}, bf16[256,256]{1,0:T(8,128)(2,1)S(1)}, u32[]{:S(2)}, u32[]{:S(2)}) %collective-permute-start.5) | collective-permute-done | bytes 131104 | tf_op jit(solution)/shard_map/ppermute | solution.py:109
  88.6 3.6 %collective-permute-done.4 = bf16[256,256]{1,0:T(8,128)(2,1)S(1)} collective-permute-done((bf16[256,256]{1,0:T(8,128)(2,1)S(1)}, bf16[256,256]{1,0:T(8,128)(2,1)S(1)}, u32[]{:S(2)}, u32[]{:S(2)}) %collective-permute-start.4) | collective-permute-done | bytes 131104 | tf_op jit(solution)/shard_map/ppermute | solution.py:109
  92.2 0.1 fusion.2
  92.3 8.1 %all_to_all.19 = bf16[8,32,256]{2,1,0:T(8,128)(2,1)S(1)} all-to-all(bf16[8,32,256]{2,1,0:T(8,128)(2,1)S(1)} %bitcast.44), channel_id=1, replica_groups=mesh['ctx'=4,'exp'=8] {'exp'}, dimensions={0} | all-to-all | bytes 262144 | tf_op jit(solution)/shard_map/all_to_all | solution.py:112
  100.4 0.1 reduce
  100.6 0.6 copy.52
  101.3 0.6 copy.53
  101.9 1.6 %copy-done.1 = bf16[512,2048]{1,0:T(8,128)(2,1)S(1)} copy-done((bf16[512,2048]{1,0:T(8,128)(2,1)S(1)}, bf16[512,2048]{1,0:T(8,128)(2,1)}, u32[]{:S(2)}) %copy-start.1) | copy-done | bytes 2097176
  103.5 7.0 %tiles.2.rest_0_ = f32[768,4096]{1,0:T(8,128)} custom-call(bf16[768,1024]{1,0:T(8,128)(2,1)S(1)} %weighted.1.weight_ref, bf16[512,2048]{1,0:T(8,128)(2,1)S(1)} %copy-done.1, bf16[512,2048]{1,0:T(8,128)(2,1)} %collective-permute-done.6.second_ref), custom_call_target="tpu_custom_call" | custom-call | tf_op jit(solution)/shard_map/tiles/pallas_call | solution.py:193
  110.5 5.5 %tiles.3 = f32[768,4096]{1,0:T(8,128)} custom-call(bf16[768,1024]{1,0:T(8,128)(2,1)S(1)} %weighted.1.weight_ref, bf16[512,2048]{1,0:T(8,128)(2,1)S(1)} %copy-done.2, bf16[512,2048]{1,0:T(8,128)(2,1)S(1)} %collective-permute-done.7.second_ref, f32[768,4096]{1,0:T(8,128)} %tiles.2.rest_0_), custom_call_target="tpu_custom_call", output_to_operand_aliasing={{}: (3, {})} | custom-call | tf_op jit(solution)/shard_map/tiles/pallas_call | solution.py:193
  (43 shorter events, 0.4 us)
Async XLA Ops:
  7.2 54.7 %copy-start = (s32[4,4]{1,0:T(4,128)S(1)}, s32[4,4]{1,0:T(4,128)}, u32[]{:S(2)}) copy-start(s32[4,4]{1,0:T(4,128)} %param.18) | copy-start | bytes 196
  7.2 3.2 %copy-start.10 = (bf16[128,8]{0,1:T(8,128)(2,1)S(1)}, bf16[128,8]{0,1:T(8,128)(2,1)}, u32[]{:S(2)}) copy-start(bf16[128,8]{0,1:T(8,128)(2,1)} %param.20) | copy-start | bytes 6148
  7.2 3.2 %copy-start.9 = (s32[128,8]{0,1:T(8,128)S(1)}, s32[128,8]{0,1:T(8,128)}, u32[]{:S(2)}) copy-start(s32[128,8]{0,1:T(8,128)} %param.19) | copy-start | bytes 12292
  7.2 3.3 %copy-start.7 = (bf16[1,3,8,65,384]{4,2,3,1,0:T(8,128)(2,1)S(1)}, bf16[1,3,8,65,384]{4,2,3,1,0:T(8,128)(2,1)}, u32[]{:S(2)}) copy-start(bf16[1,3,8,65,384]{4,2,3,1,0:T(8,128)(2,1)} %param.23) | copy-start | bytes 3594244
  7.2 44.1 %all-gather.5.cloned.1.call-start = ((), (), s32[]{:S(2)}) async-start(), calls=%async_computation.4 | async-start | bytes 2621440 | tf_op jit(solution)/shard_map/all_gather | solution.py:220
  9.7 92.2 %all-gather.3.cloned.1.call-start = ((), (), s32[]{:S(2)}) async-start(), calls=%async_computation.3 | async-start | bytes 2621440 | tf_op jit(solution)/shard_map/all_gather | solution.py:220
  10.5 6.3 %copy-start.11 = (s32[16]{0:T(128)S(1)}, s32[16]{0:T(128)}, u32[]{:S(2)}) copy-start(s32[16]{0:T(128)} %param.22) | copy-start | bytes 196
  11.6 15.7 %all-to-all-start.1 = ((bf16[8,65,384]{2,1,0:T(8,128)(2,1)}), bf16[8,65,384]{2,1,0:T(8,128)(2,1)S(1)}, u32[]{:S(2)}, u32[]{:S(2)}) async-start(bf16[8,65,384]{2,1,0:T(8,128)(2,1)} %pad_maximum_fusion.1), calls=%async_computation.1 | async-start | bytes 884736 | tf_op jit(solution)/shard_map/all_to_all | solution.py:232
  28.7 22.6 %copy-start.8 = (bf16[256,256]{1,0:T(8,128)(2,1)S(1)}, bf16[256,256]{1,0:T(8,128)(2,1)}, u32[]{:S(2)}) copy-start(bf16[256,256]{1,0:T(8,128)(2,1)} %param.14) | copy-start | bytes 393220
  28.7 13.6 %all-to-all-start.2 = ((bf16[8,64,384]{2,1,0:T(8,128)(2,1)}), bf16[8,64,384]{2,1,0:T(8,128)(2,1)S(1)}, u32[]{:S(2)}, u32[]{:S(2)}) async-start(bf16[8,64,384]{2,1,0:T(8,128)(2,1)} %gather_fusion.1), calls=%async_computation.2 | async-start | bytes 786432 | tf_op jit(solution)/shard_map/all_to_all | solution.py:241
  32.5 34.0 %copy-start.6 = (f32[4,256]{1,0:T(4,128)S(1)}, f32[4,256]{1,0:T(4,128)}, u32[]{:S(2)}) copy-start(f32[4,256]{1,0:T(4,128)} %lse_ref.1) | copy-start | bytes 12292
  51.3 50.6 %collective-permute-start.6 = (bf16[512,2048]{1,0:T(8,128)(2,1)}, bf16[512,2048]{1,0:T(8,128)(2,1)}, u32[]{:S(2)}, u32[]{:S(2)}) collective-permute-start(bf16[512,2048]{1,0:T(8,128)(2,1)} %all-gather.5.cloned.1.call-done.first_ref), channel_id=1, source_target_pairs={{0,1},{1,0},{2,3},{3,2},{4,5},{5,4},{6,7},{7,6},{8,9},{9,8},{10,11... | collective-permute-start | bytes 6291464 | tf_op jit(solution)/shard_map/ppermute | solution.py:257
  52.2 10.3 %collective-permute-start.1 = (bf16[256,256]{1,0:T(8,128)(2,1)S(1)}, bf16[256,256]{1,0:T(8,128)(2,1)S(1)}, u32[]{:S(2)}, u32[]{:S(2)}) collective-permute-start(bf16[256,256]{1,0:T(8,128)(2,1)S(1)} %get-tuple-element.18), channel_id=1, source_target_pairs={{0,16},{8,24},{1,17},{9,25},{2,18},{10,26},{3,19},{11,27},{4,20},{... | collective-permute-start | bytes 393224 | tf_op jit(solution)/shard_map/ppermute | solution.py:89
  56.9 7.4 %collective-permute-start = (bf16[256,256]{1,0:T(8,128)(2,1)S(1)}, bf16[256,256]{1,0:T(8,128)(2,1)S(1)}, u32[]{:S(2)}, u32[]{:S(2)}) collective-permute-start(bf16[256,256]{1,0:T(8,128)(2,1)S(1)} %get-tuple-element.18), channel_id=1, source_target_pairs={{0,8},{8,16},{16,24},{1,9},{9,17},{17,25},{2,10},{10,18},{18,26},{... | collective-permute-start | bytes 393224 | tf_op jit(solution)/shard_map/ppermute | solution.py:89
  60.5 5.9 %collective-permute-start.2 = (bf16[256,256]{1,0:T(8,128)(2,1)S(1)}, bf16[256,256]{1,0:T(8,128)(2,1)S(1)}, u32[]{:S(2)}, u32[]{:S(2)}) collective-permute-start(bf16[256,256]{1,0:T(8,128)(2,1)S(1)} %get-tuple-element.18), channel_id=1, source_target_pairs={{0,24},{1,25},{2,26},{3,27},{4,28},{5,29},{6,30},{7,31}} | collective-permute-start | bytes 393224 | tf_op jit(solution)/shard_map/ppermute | solution.py:89
  66.5 1.0 copy-start.3
  67.4 0.9 copy-start.4
  68.4 0.9 copy-start.5
  72.4 9.4 %collective-permute-start.3 = (bf16[256,256]{1,0:T(8,128)(2,1)S(1)}, bf16[256,256]{1,0:T(8,128)(2,1)S(1)}, u32[]{:S(2)}, u32[]{:S(2)}) collective-permute-start(bf16[256,256]{1,0:T(8,128)(2,1)S(1)} %get-tuple-element.14), channel_id=1, source_target_pairs={{8,0},{16,8},{24,16},{9,1},{17,9},{25,17},{10,2},{18,10},{26,18},{... | collective-permute-start | bytes 393224 | tf_op jit(solution)/shard_map/ppermute | solution.py:109
  73.7 15.0 %collective-permute-start.5 = (bf16[256,256]{1,0:T(8,128)(2,1)S(1)}, bf16[256,256]{1,0:T(8,128)(2,1)S(1)}, u32[]{:S(2)}, u32[]{:S(2)}) collective-permute-start(bf16[256,256]{1,0:T(8,128)(2,1)S(1)} %get-tuple-element.15), channel_id=1, source_target_pairs={{24,0},{25,1},{26,2},{27,3},{28,4},{29,5},{30,6},{31,7}} | collective-permute-start | bytes 393224 | tf_op jit(solution)/shard_map/ppermute | solution.py:109
  75.0 17.2 %collective-permute-start.4 = (bf16[256,256]{1,0:T(8,128)(2,1)S(1)}, bf16[256,256]{1,0:T(8,128)(2,1)S(1)}, u32[]{:S(2)}, u32[]{:S(2)}) collective-permute-start(bf16[256,256]{1,0:T(8,128)(2,1)S(1)} %get-tuple-element.16), channel_id=1, source_target_pairs={{16,0},{24,8},{17,1},{25,9},{18,2},{26,10},{19,3},{27,11},{20,4},{... | collective-permute-start | bytes 393224 | tf_op jit(solution)/shard_map/ppermute | solution.py:109
  101.9 8.6 %collective-permute-start.7 = (bf16[512,2048]{1,0:T(8,128)(2,1)}, bf16[512,2048]{1,0:T(8,128)(2,1)S(1)}, u32[]{:S(2)}, u32[]{:S(2)}) collective-permute-start(bf16[512,2048]{1,0:T(8,128)(2,1)} %all-gather.3.cloned.1.call-done.first_ref), channel_id=1, source_target_pairs={{0,1},{1,0},{2,3},{3,2},{4,5},{5,4},{6,7},{7,6},{8,9},{9,8},{10,11... | collective-permute-start | bytes 6291464 | tf_op jit(solution)/shard_map/ppermute | solution.py:257
  101.9 1.6 %copy-start.1 = (bf16[512,2048]{1,0:T(8,128)(2,1)S(1)}, bf16[512,2048]{1,0:T(8,128)(2,1)}, u32[]{:S(2)}) copy-start(bf16[512,2048]{1,0:T(8,128)(2,1)} %all-gather.5.cloned.1.call-done.first_ref) | copy-start | bytes 6291460
  103.5 7.0 %copy-start.2 = (bf16[512,2048]{1,0:T(8,128)(2,1)S(1)}, bf16[512,2048]{1,0:T(8,128)(2,1)}, u32[]{:S(2)}) copy-start(bf16[512,2048]{1,0:T(8,128)(2,1)} %all-gather.3.cloned.1.call-done.first_ref) | copy-start | bytes 6291460
Sparse Core Ops, SparseCore 0:
  10.5 40.7 all-gather.4
  53.1 35.8 all-gather.2

commit v3 on v2

--- a/solution.py
+++ b/solution.py
@@ -13,13 +13,19 @@
 
 
 def attention_kernel(
-    live_ref, query_ref, grad_ref, out_ref, lse_ref, pairs_ref, query_grad_ref, terms_ref, sums_ref
+    place_ref, mask_ref, query_ref, grad_ref, out_ref, lse_ref, *rest
 ):
+    cycle = mask_ref.shape[0]
+    pair_refs, (query_grad_ref, terms_ref, sums_ref, pairs_ref) = rest[:cycle], rest[cycle:]
     rows, width = pairs_ref.shape[1], pairs_ref.shape[2] // 2
     heads = lse_ref.shape[0]
+    kv_count = terms_ref.shape[2] // (2 * width)
     scale = 1.0 / math.sqrt(width)
+    mine, kv_head = place_ref[0], place_ref[1]
     offset = 0.5 * math.log(rows) + lse_ref[...]
     spans = [slice(h * width, (h + 1) * width) for h in range(heads)]
+    for step, pair_ref in enumerate(pair_refs):
+        pairs_ref[step] = pair_ref[...]
     delta = []
     for span in spans:
         both = grad_ref[:, span].astype(jnp.float32) * out_ref[:, span].astype(jnp.float32)
@@ -47,24 +53,32 @@
                 sums_ref[:, span] += query_term
         queries = jnp.concatenate([query_ref[:, span] for span in spans], axis=0)
         grads = jnp.concatenate([grad_ref[:, span] for span in spans], axis=0)
-        terms_ref[step, :, :width] = jnp.dot(
+        key_term = jnp.dot(
             jnp.concatenate(slopes, axis=1), queries, preferred_element_type=jnp.float32
-        ).astype(jnp.bfloat16)
-        terms_ref[step, :, width:] = jnp.dot(
+        )
+        value_term = jnp.dot(
             jnp.concatenate(probs, axis=1), grads, preferred_element_type=jnp.float32
-        ).astype(jnp.bfloat16)
+        )
+        for n, term in enumerate((key_term, value_term)):
+            for k in range(kv_count):
+                at = (n * kv_count + k) * width
+                terms_ref[mine - step, :, at : at + width] = jnp.where(
+                    kv_head == k, term, 0.0
+                ).astype(jnp.bfloat16)
 
     block(0, True)
 
-    @pl.loop(1, pairs_ref.shape[0])
-    def _(step):
-        @pl.when(live_ref[step] > 0)
+    @pl.loop(0, cycle)
+    def _(source):
+        seen = jnp.logical_and(source < mine, mask_ref[mine, source] > 0)
+
+        @pl.when(seen)
         def _():
-            block(step, False)
-
-        @pl.when(live_ref[step] <= 0)
+            block(mine - source, False)
+
+        @pl.when(jnp.logical_and(source != mine, jnp.logical_not(seen)))
         def _():
-            terms_ref[step] = jnp.zeros_like(terms_ref[step])
+            terms_ref[source] = jnp.zeros_like(terms_ref[source])
 
     query_grad_ref[...] = sums_ref[...].astype(jnp.bfloat16)
 
@@ -89,36 +103,38 @@
         lax.ppermute(pair, "ctx", [(c, c + step) for c in range(cycle - step)])
         for step in range(1, cycle)
     ]
-    source = mine - jnp.arange(cycle, dtype=jnp.int32)
-    live = jnp.where(source >= 0, block_mask[mine, jnp.maximum(source, 0)], 0)
     whole = pl.BlockSpec(memory_space=pltpu.VMEM)
+    scalars = pl.BlockSpec(memory_space=pltpu.SMEM)
     query_grad, terms = pl.pallas_call(
         attention_kernel,
         out_shape=(
             jax.ShapeDtypeStruct(queries.shape, jnp.bfloat16),
-            jax.ShapeDtypeStruct((cycle, rows, 2 * width), jnp.bfloat16),
+            jax.ShapeDtypeStruct((cycle, rows, 2 * kv_count * width), jnp.bfloat16),
         ),
-        in_specs=[pl.BlockSpec(memory_space=pltpu.SMEM)] + [whole] * 5,
+        in_specs=[scalars] * 2 + [whole] * (4 + cycle),
         out_specs=(whole, whole),
-        scratch_shapes=[pltpu.VMEM(queries.shape, jnp.float32)],
+        scratch_shapes=[
+            pltpu.VMEM(queries.shape, jnp.float32),
+            pltpu.VMEM((cycle,) + pair.shape, jnp.bfloat16),
+        ],
         compiler_params=pltpu.CompilerParams(vmem_limit_bytes=40 * 2**20),
         name="attention",
-    )(live, queries, attn_out_grad, attn_out, lse_excess, jnp.stack(arrived))
-    total = terms[0].astype(jnp.float32)
-    for step in range(1, cycle):
-        total = total + lax.ppermute(
-            terms[step], "ctx", [(c, c - step) for c in range(step, cycle)]
-        ).astype(jnp.float32)
-    parts = lax.all_to_all(
-        total.astype(jnp.bfloat16), "exp", split_axis=0, concat_axis=0, tiled=True
-    )
-    kv_sum = jnp.sum(
-        parts.reshape(kv_count, owners // kv_count, rows // owners, 2, width).astype(jnp.float32),
-        axis=1,
-    )
-    final = jnp.transpose(kv_sum, (2, 1, 0, 3)).reshape(2, rows // owners, kv_count * width)
-    final = final.astype(jnp.bfloat16)
-    return (query_grad, final[0], final[1])
+    )(
+        jnp.stack([mine, kv_head]).astype(jnp.int32),
+        block_mask,
+        queries,
+        attn_out_grad,
+        attn_out,
+        lse_excess,
+        *arrived,
+    )
+    total = lax.psum_scatter(
+        terms.reshape(cycle * rows, 2 * kv_count * width),
+        ("ctx", "exp"),
+        scatter_dimension=0,
+        tiled=True,
+    )
+    return query_grad, total
 
 
 def weight_kernel(order_ref, flag_ref, probs_ref, hidden_ref, shadow_ref, weight_ref):
@@ -211,7 +227,8 @@
     per_dev = count // owners
     units = stored_hidden_state.shape[4]
     chips = owners // 2
-    alike = [[2 * chip + core for chip in range(chips)] for core in range(2)]
+    ring = [chip ^ (chip >> 1) for chip in range(chips)]
+    alike = [[2 * chip for chip in ring], [2 * chip + 1 for chip in ring[::-1]]]
     swap = functools.partial(
         lax.all_to_all, axis_name="exp", split_axis=0, concat_axis=0, tiled=True
     )
@@ -240,8 +257,11 @@
     hosts = jnp.max(shadow_list.reshape(owners, per_dev), axis=1)
     shadow_rows = swap(mixed[:, :limit][hosts])
     flags = lax.dynamic_slice_in_dim(shadow_list, own_index * per_dev, per_dev) >= 0
-    place = jnp.arange(owners, dtype=jnp.int32)
-    order = 2 * (place % chips) + (place // chips + own_index) % 2
+    order = jnp.where(
+        own_index % 2 == 0,
+        jnp.array(alike[0] + alike[1], jnp.int32),
+        jnp.array(alike[1] + alike[0], jnp.int32),
+    )
     weighted = weighted_rows(
         probs, stored_hidden_state, shadow_rows, flags.astype(jnp.int32), order
     )
@@ -277,14 +297,16 @@
     shadow_list,
     stored_hidden_state,
 ):
-    query_grad, key_grad, value_grad = attention(
+    query_grad, kv_grad = attention(
         queries, keys, values, attn_out, attn_out_grad, lse_excess, block_mask
     )
     weighted, gathered = experts(
         expert_ids, route_probs, moe_grad, shadow_list, stored_hidden_state
     )
     per_dev = shadow_list.shape[0] // lax.axis_size("exp")
-    expert_grad = expert_tiles(weighted, gathered, (weighted, (key_grad, value_grad)), per_dev)
+    expert_grad = expert_tiles(weighted, gathered, ((weighted, query_grad), None), per_dev)
+    kv_grad, expert_grad = lax.optimization_barrier((kv_grad, expert_grad))
+    key_grad, value_grad = jnp.split(kv_grad, 2, axis=1)
     return (query_grad, key_grad, value_grad, expert_grad)
 
 

time: 124 us -> 221 us (1.78)
  waiting for transfers between devices: 45.4 us -> 155 us
  blocking collectives: 8.07 us -> 0 us
  starting transfers between devices: 22.3 us -> 18.3 us
  local copies, waits for them, and re-layouts: 11.5 us -> 9.01 us
    reduce_scatter x0 -> x1, waiting for transfers between devices: none -> 119 us  [attention(): lax.psum_scatter(terms.reshape(cycle * rows, 2 * kv_count * width), ('ctx...]
    all_gather x2, waiting for transfers between devices: 4.63 us -> 25.6 us  [experts(): lax.all_gather(columns, 'exp', axis_index_groups=alike, tiled=True)]
    ppermute x3 -> x0, waiting for transfers between devices: 15.9 us -> none  [attention(): lax.ppermute(terms[step], 'ctx', [(c, c - step) for c in range(step, cycl...]
    all_to_all x1, waiting for transfers between devices: 10.3 us -> 1.46 us  [experts(): swap(jnp.concatenate([stored_hidden_state[0, per_dev, :, :limit], table.r...]
    all_to_all x1 -> x0, blocking collectives: 8.07 us -> none  [attention(): lax.all_to_all(total.astype(jnp.bfloat16), 'exp', split_axis=0, concat_ax...]
    ppermute x3, waiting for transfers between devices: 3.93 us -> 0.01 us  [attention(): lax.ppermute(pair, 'ctx', [(c, c + step) for c in range(cycle - step)])]
    ppermute x3 -> x0, starting transfers between devices: 3.88 us -> none  [attention(): lax.ppermute(terms[step], 'ctx', [(c, c - step) for c in range(step, cycl...]
    unnamed x28 -> x36, local copies, waits for them, and re-layouts: 5.87 us -> 2.88 us
  transfers between devices with their start and end apart: 12 -> 10, of which waited for: 8 -> 4; matrix products, arithmetic and copies ran while one was open for 5% -> 2% of each run, Pallas kernels for 12% -> 10%
where the time goes in v3:
time: 221 us; the launch traced here: 220 us
  waiting for transfers between devices  155 us (70%)
  Pallas kernels  21.3 us (10%)
  starting transfers between devices  18.3 us (8%)
  between operations  15.9 us (7%)
  local copies, waits for them, and re-layouts  9.01 us (4%)
    reduce_scatter x1, waiting for transfers between devices, attention(): lax.psum_scatter(terms.reshape(cycle * rows, 2 * kv_count * width), ('ctx...  119 us
    all_gather x2, waiting for transfers between devices, experts(): lax.all_gather(columns, 'exp', axis_index_groups=alike, tiled=True)  25.6 us
    pallas_call x2, Pallas kernels, tile_columns(): pl.pallas_call(tile_kernel, out_shape=jax.ShapeDtypeStruct((rows, width),...  13.9 us
    ppermute x3, starting transfers between devices, attention(): lax.ppermute(pair, 'ctx', [(c, c + step) for c in range(cycle - step)])  9.28 us
    all_to_all x1, waiting for transfers between devices, experts(): shadow_rows = swap(mixed[:, :limit][hosts])  7.51 us
    all_to_all x1, starting transfers between devices, experts(): swap(jnp.concatenate([stored_hidden_state[0, per_dev, :, :limit], table.r...  5.31 us
  transfers between devices with their start and end apart: 10, of which 4 were waited for; matrix products, arithmetic and copies ran while one was open for 2% of the time, Pallas kernels for 10%

profile of v3, /device:TPU:0, one launch (start us, length us, event | category | flops | bytes accessed | tf_op | source)
XLA Modules:
  0.0 220.3 jit_solution(11862085600250566659)
XLA Ops:
  8.0 0.0 copy-start.13
  8.0 0.0 all-gather.5.cloned.1.call-start
  8.1 2.4 %fusion.1 = (bf16[128,2048]{1,0:T(8,128)(2,1)}, bf16[128,2048]{1,0:T(8,128)(2,1)}) fusion(bf16[128,4096]{1,0:T(8,128)(2,1)} %param.23), kind=kLoop, calls=%fused_computation.17 | loop fusion | bytes 2097152 | tf_op jit(solution)/shard_map/split | solution.py:238
  10.5 0.0 all-gather.5.cloned.1.call-update
  10.5 0.0 all-gather.3.cloned.1.call-start
  10.5 0.7 all-gather.3.cloned.1.call-update
  11.4 0.0 copy-start.10
  11.4 0.0 copy-start.11
  11.4 0.2 copy.31.hidden_ref
  11.6 0.0 copy-start.14
  11.6 0.8 pad_maximum_fusion
  12.5 0.0 copy-start.5
  12.5 0.0 copy-start.6
  12.5 0.0 copy-start.7
  12.5 5.3 %all-to-all-start = ((bf16[8,65,384]{2,1,0:T(8,128)(2,1)}), bf16[8,65,384]{2,1,0:T(8,128)(2,1)S(1)}, u32[]{:S(2)}, u32[]{:S(2)}) async-start(bf16[8,65,384]{2,1,0:T(8,128)(2,1)} %pad_maximum_fusion), calls=%async_computation.1 | async-start | bytes 884736 | tf_op jit(solution)/shard_map/all_to_all | solution.py:249
  17.9 5.5 %collective-permute-start.2 = (bf16[256,256]{1,0:T(8,128)(2,1)S(1)}, bf16[256,256]{1,0:T(8,128)(2,1)S(1)}, u32[]{:S(2)}, u32[]{:S(2)}) collective-permute-start(bf16[256,256]{1,0:T(8,128)(2,1)S(1)} %pad_maximum_fusion.1.rest_0_), channel_id=1, source_target_pairs={{0,24},{1,25},{2,26},{3,27},{4,28},{5,29},{6,30},{7,31}} | collective-permute-start | bytes 393224 | tf_op jit(solution)/shard_map/ppermute | solution.py:103
  23.4 1.3 collective-permute-start.1
  24.7 2.5 %collective-permute-start = (bf16[256,256]{1,0:T(8,128)(2,1)S(1)}, bf16[256,256]{1,0:T(8,128)(2,1)S(1)}, u32[]{:S(2)}, u32[]{:S(2)}) collective-permute-start(bf16[256,256]{1,0:T(8,128)(2,1)S(1)} %pad_maximum_fusion.1.rest_0_), channel_id=1, source_target_pairs={{0,8},{8,16},{16,24},{1,9},{9,17},{17,25},{2,10},{10,18},{18,26},{... | collective-permute-start | bytes 393224 | tf_op jit(solution)/shard_map/ppermute | solution.py:103
  27.2 0.0 copy-done.14
  27.2 0.1 reshape.50
  27.3 0.1 reduce_max.11
  27.4 1.5 all-to-all-done
  29.0 1.4 gather_fusion
  30.3 3.5 %all-to-all-start.1 = ((bf16[8,64,384]{2,1,0:T(8,128)(2,1)}), bf16[8,64,384]{2,1,0:T(8,128)(2,1)S(1)}, u32[]{:S(2)}, u32[]{:S(2)}) async-start(bf16[8,64,384]{2,1,0:T(8,128)(2,1)} %gather_fusion), calls=%async_computation.2 | async-start | bytes 786432 | tf_op jit(solution)/shard_map/all_to_all | solution.py:258
  33.8 0.0 reduce-scatter.2.cloned.1.call-start
  33.9 0.1 compare_convert_fusion.flag_ref
  33.9 0.1 pad_add_fusion.place_ref
  34.0 0.0 collective-permute-done.2.rest_3_
  34.0 0.0 collective-permute-done.1.rest_2_
  34.0 0.0 collective-permute-done.rest_1_
  34.1 3.1 %attention.1 = (bf16[256,512]{1,0:T(8,128)(2,1)}, bf16[4,256,512]{2,1,0:T(8,128)(2,1)S(1)}) custom-call(s32[2]{0:T(128)S(1)} %pad_add_fusion.place_ref, s32[4,4]{1,0:T(4,128)S(1)} %copy-done.7, bf16[256,512]{1,0:T(8,128)(2,1)S(1)} %copy-done.3, bf16[256,512]{1,0:T(8,128)(2,1)S(1)} %copy-done.4, bf16[256,512]{1,0:T(8,128)(2,1)S(1)} %copy-done.5, ...), custom_call_target="tpu_custom_call" | custom-call | tf_op jit(solution)/shard_map/attention/pallas_call | solution.py:108
  37.2 1.0 copy-done.2
  38.2 0.8 slice.19
  39.1 7.5 %all-to-all-done.1.shadow_ref = bf16[8,64,384]{2,1,0:T(8,128)(2,1)S(1)} async-done(((bf16[8,64,384]{2,1,0:T(8,128)(2,1)}), bf16[8,64,384]{2,1,0:T(8,128)(2,1)S(1)}, u32[]{:S(2)}, u32[]{:S(2)}) %all-to-all-start.1) | async-done | bytes 393248 | tf_op jit(solution)/shard_map/all_to_all | solution.py:258
  46.6 4.3 %weighted.1.weight_ref = bf16[768,1024]{1,0:T(8,128)(2,1)S(1)} custom-call(s32[8]{0:T(128)S(1)} %broadcast_select_fusion.order_ref, s32[2]{0:T(128)S(1)} %compare_convert_fusion.flag_ref, bf16[8,2,128]{2,1,0:T(2,128)(2,1)S(1)} %reshape.49.probs_ref, bf16[1,3,8,65,384]{4,3,2,1,0:T(8,128)(2,1)S(1)} %copy.31.hidden_ref, ...), custom_call_target="tpu_custom_call" | custom-call | tf_op jit(solution)/shard_map/weighted/pallas_call | solution.py:171
  50.9 0.0 all-gather.5.cloned.1.call-done.first_ref
  50.9 0.1 collective-permute-start.3
  51.0 25.6 %all-gather.3.cloned.1.call-done.first_ref = bf16[512,2048]{1,0:T(8,128)(2,1)} async-done(((bf16[128,2048]{1,0:T(8,128)(2,1)}), bf16[512,2048]{1,0:T(8,128)(2,1)}) %all-gather.3.cloned.1.call-update) | async-done | bytes 2097168 | tf_op jit(solution)/shard_map/all_gather | solution.py:237
  76.6 0.0 collective-permute-done.3.second_ref
  76.6 0.0 collective-permute-start.4
  76.6 0.0 reduce-scatter.2.cloned.1.call-update
  76.7 1.6 copy-done
  78.3 7.0 %tiles.2.rest_0_ = f32[768,4096]{1,0:T(8,128)} custom-call(bf16[768,1024]{1,0:T(8,128)(2,1)S(1)} %weighted.1.weight_ref, bf16[512,2048]{1,0:T(8,128)(2,1)S(1)} %copy-done, bf16[512,2048]{1,0:T(8,128)(2,1)} %collective-permute-done.3.second_ref), custom_call_target="tpu_custom_call" | custom-call | tf_op jit(solution)/shard_map/tiles/pallas_call | solution.py:209
  85.3 0.0 collective-permute-done.4.second_ref
  85.3 0.0 copy-done.1
  85.3 6.9 %tiles.3 = f32[768,4096]{1,0:T(8,128)} custom-call(bf16[768,1024]{1,0:T(8,128)(2,1)S(1)} %weighted.1.weight_ref, bf16[512,2048]{1,0:T(8,128)(2,1)S(1)} %copy-done.1, bf16[512,2048]{1,0:T(8,128)(2,1)} %collective-permute-done.4.second_ref, f32[768,4096]{1,0:T(8,128)} %tiles.2.rest_0_), custom_call_target="tpu_custom_call", output_to_operand_aliasing={{}: (3, {})} | custom-call | tf_op jit(solution)/shard_map/tiles/pallas_call | solution.py:209
  92.1 119.4 %reduce-scatter.2.cloned.1.call-done = bf16[32,512]{1,0:T(8,128)(2,1)} async-done(((bf16[1024,512]{1,0:T(8,128)(2,1)}), bf16[32,512]{1,0:T(8,128)(2,1)}) %reduce-scatter.2.cloned.1.call-update) | async-done | bytes 32784 | tf_op jit(solution)/shard_map/reduce_scatter | solution.py:131
  211.5 1.3 fusion.2
  (38 shorter events, 0.3 us)
Async XLA Ops:
  8.0 3.3 %copy-start.13 = (bf16[128,8]{0,1:T(8,128)(2,1)S(1)}, bf16[128,8]{0,1:T(8,128)(2,1)}, u32[]{:S(2)}) copy-start(bf16[128,8]{0,1:T(8,128)(2,1)} %param.22) | copy-start | bytes 6148
  8.0 3.3 %copy-start.12 = (s32[128,8]{0,1:T(8,128)S(1)}, s32[128,8]{0,1:T(8,128)}, u32[]{:S(2)}) copy-start(s32[128,8]{0,1:T(8,128)} %param.21) | copy-start | bytes 12292
  8.0 3.3 %copy-start.9 = (bf16[1,3,8,65,384]{4,2,3,1,0:T(8,128)(2,1)S(1)}, bf16[1,3,8,65,384]{4,2,3,1,0:T(8,128)(2,1)}, u32[]{:S(2)}) copy-start(bf16[1,3,8,65,384]{4,2,3,1,0:T(8,128)(2,1)} %param.25) | copy-start | bytes 3594244
  8.0 42.9 %all-gather.5.cloned.1.call-start = ((), (), s32[]{:S(2)}) async-start(), calls=%async_computation.5 | async-start | bytes 2621440 | tf_op jit(solution)/shard_map/all_gather | solution.py:237
  10.5 66.1 %all-gather.3.cloned.1.call-start = ((), (), s32[]{:S(2)}) async-start(), calls=%async_computation.4 | async-start | bytes 2621440 | tf_op jit(solution)/shard_map/all_gather | solution.py:237
  11.4 6.5 %copy-start.10 = (bf16[256,256]{1,0:T(8,128)(2,1)S(1)}, bf16[256,256]{1,0:T(8,128)(2,1)}, u32[]{:S(2)}) copy-start(bf16[256,256]{1,0:T(8,128)(2,1)} %param.16) | copy-start | bytes 393220
  11.4 6.5 %copy-start.11 = (bf16[256,256]{1,0:T(8,128)(2,1)S(1)}, bf16[256,256]{1,0:T(8,128)(2,1)}, u32[]{:S(2)}) copy-start(bf16[256,256]{1,0:T(8,128)(2,1)} %param.15) | copy-start | bytes 393220
  11.6 15.6 %copy-start.14 = (s32[16]{0:T(128)S(1)}, s32[16]{0:T(128)}, u32[]{:S(2)}) copy-start(s32[16]{0:T(128)} %param.24) | copy-start | bytes 196
  12.5 21.4 %copy-start.15 = (s32[8]{0:T(128)S(1)}, s32[8]{0:T(128)}, u32[]{:S(2)}) copy-start(s32[8]{0:T(128)} %constant.57.clone) | copy-start | bytes 100
  12.5 21.4 %copy-start.16 = (s32[8]{0:T(128)S(1)}, s32[8]{0:T(128)}, u32[]{:S(2)}) copy-start(s32[8]{0:T(128)} %constant.56.clone) | copy-start | bytes 100
  12.5 21.6 %copy-start.3 = (bf16[256,512]{1,0:T(8,128)(2,1)S(1)}, bf16[256,512]{1,0:T(8,128)(2,1)}, u32[]{:S(2)}) copy-start(bf16[256,512]{1,0:T(8,128)(2,1)} %query_ref.1) | copy-start | bytes 786436
  12.5 21.6 %copy-start.4 = (bf16[256,512]{1,0:T(8,128)(2,1)S(1)}, bf16[256,512]{1,0:T(8,128)(2,1)}, u32[]{:S(2)}) copy-start(bf16[256,512]{1,0:T(8,128)(2,1)} %grad_ref.1) | copy-start | bytes 786436
  12.5 21.6 %copy-start.5 = (bf16[256,512]{1,0:T(8,128)(2,1)S(1)}, bf16[256,512]{1,0:T(8,128)(2,1)}, u32[]{:S(2)}) copy-start(bf16[256,512]{1,0:T(8,128)(2,1)} %out_ref.1) | copy-start | bytes 786436
  12.5 21.6 %copy-start.6 = (f32[4,256]{1,0:T(4,128)S(1)}, f32[4,256]{1,0:T(4,128)}, u32[]{:S(2)}) copy-start(f32[4,256]{1,0:T(4,128)} %lse_ref.1) | copy-start | bytes 12292
  12.5 21.6 %copy-start.7 = (s32[4,4]{1,0:T(4,128)S(1)}, s32[4,4]{1,0:T(4,128)}, u32[]{:S(2)}) copy-start(s32[4,4]{1,0:T(4,128)} %mask_ref.1) | copy-start | bytes 196
  12.5 16.4 %all-to-all-start = ((bf16[8,65,384]{2,1,0:T(8,128)(2,1)}), bf16[8,65,384]{2,1,0:T(8,128)(2,1)S(1)}, u32[]{:S(2)}, u32[]{:S(2)}) async-start(bf16[8,65,384]{2,1,0:T(8,128)(2,1)} %pad_maximum_fusion), calls=%async_computation.1 | async-start | bytes 884736 | tf_op jit(solution)/shard_map/all_to_all | solution.py:249
  17.9 16.1 %collective-permute-start.2 = (bf16[256,256]{1,0:T(8,128)(2,1)S(1)}, bf16[256,256]{1,0:T(8,128)(2,1)S(1)}, u32[]{:S(2)}, u32[]{:S(2)}) collective-permute-start(bf16[256,256]{1,0:T(8,128)(2,1)S(1)} %pad_maximum_fusion.1.rest_0_), channel_id=1, source_target_pairs={{0,24},{1,25},{2,26},{3,27},{4,28},{5,29},{6,30},{7,31}} | collective-permute-start | bytes 393224 | tf_op jit(solution)/shard_map/ppermute | solution.py:103
  23.4 10.6 %collective-permute-start.1 = (bf16[256,256]{1,0:T(8,128)(2,1)S(1)}, bf16[256,256]{1,0:T(8,128)(2,1)S(1)}, u32[]{:S(2)}, u32[]{:S(2)}) collective-permute-start(bf16[256,256]{1,0:T(8,128)(2,1)S(1)} %pad_maximum_fusion.1.rest_0_), channel_id=1, source_target_pairs={{0,16},{8,24},{1,17},{9,25},{2,18},{10,26},{3,19},{11,27},{4,20},{... | collective-permute-start | bytes 393224 | tf_op jit(solution)/shard_map/ppermute | solution.py:103
  24.7 9.3 %collective-permute-start = (bf16[256,256]{1,0:T(8,128)(2,1)S(1)}, bf16[256,256]{1,0:T(8,128)(2,1)S(1)}, u32[]{:S(2)}, u32[]{:S(2)}) collective-permute-start(bf16[256,256]{1,0:T(8,128)(2,1)S(1)} %pad_maximum_fusion.1.rest_0_), channel_id=1, source_target_pairs={{0,8},{8,16},{16,24},{1,9},{9,17},{17,25},{2,10},{10,18},{18,26},{... | collective-permute-start | bytes 393224 | tf_op jit(solution)/shard_map/ppermute | solution.py:103
  28.9 1.4 copy-start.8
  30.3 16.3 %all-to-all-start.1 = ((bf16[8,64,384]{2,1,0:T(8,128)(2,1)}), bf16[8,64,384]{2,1,0:T(8,128)(2,1)S(1)}, u32[]{:S(2)}, u32[]{:S(2)}) async-start(bf16[8,64,384]{2,1,0:T(8,128)(2,1)} %gather_fusion), calls=%async_computation.2 | async-start | bytes 786432 | tf_op jit(solution)/shard_map/all_to_all | solution.py:258
  33.8 177.7 %reduce-scatter.2.cloned.1.call-start = ((), (), s32[]{:S(2)}) async-start(), calls=%async_computation.3 | async-start | bytes 1081344 | tf_op jit(solution)/shard_map/reduce_scatter | solution.py:131
  37.2 1.0 copy-start.2
  50.9 25.7 %collective-permute-start.3 = (bf16[512,2048]{1,0:T(8,128)(2,1)}, bf16[512,2048]{1,0:T(8,128)(2,1)}, u32[]{:S(2)}, u32[]{:S(2)}) collective-permute-start(bf16[512,2048]{1,0:T(8,128)(2,1)} %all-gather.5.cloned.1.call-done.first_ref), channel_id=1, source_target_pairs={{0,1},{1,0},{2,3},{3,2},{4,5},{5,4},{6,7},{7,6},{8,9},{9,8},{10,11... | collective-permute-start | bytes 6291464 | tf_op jit(solution)/shard_map/ppermute | solution.py:277
  76.6 8.7 %collective-permute-start.4 = (bf16[512,2048]{1,0:T(8,128)(2,1)}, bf16[512,2048]{1,0:T(8,128)(2,1)}, u32[]{:S(2)}, u32[]{:S(2)}) collective-permute-start(bf16[512,2048]{1,0:T(8,128)(2,1)} %all-gather.3.cloned.1.call-done.first_ref), channel_id=1, source_target_pairs={{0,1},{1,0},{2,3},{3,2},{4,5},{5,4},{6,7},{7,6},{8,9},{9,8},{10,11... | collective-permute-start | bytes 6291464 | tf_op jit(solution)/shard_map/ppermute | solution.py:277
  76.7 1.6 copy-start
  78.3 7.0 %copy-start.1 = (bf16[512,2048]{1,0:T(8,128)(2,1)S(1)}, bf16[512,2048]{1,0:T(8,128)(2,1)}, u32[]{:S(2)}) copy-start(bf16[512,2048]{1,0:T(8,128)(2,1)} %all-gather.3.cloned.1.call-done.first_ref) | copy-start | bytes 6291460
Sparse Core Ops, SparseCore 0:
  11.1 36.1 all-gather.4
  48.9 27.6 all-gather.2
Sparse Core Ops, SparseCore 1:
  76.7 134.7 reduce-scatter.1

commit v4 on v3

--- a/solution.py
+++ b/solution.py
@@ -19,9 +19,8 @@
     pair_refs, (query_grad_ref, terms_ref, sums_ref, pairs_ref) = rest[:cycle], rest[cycle:]
     rows, width = pairs_ref.shape[1], pairs_ref.shape[2] // 2
     heads = lse_ref.shape[0]
-    kv_count = terms_ref.shape[2] // (2 * width)
     scale = 1.0 / math.sqrt(width)
-    mine, kv_head = place_ref[0], place_ref[1]
+    mine = place_ref[0]
     offset = 0.5 * math.log(rows) + lse_ref[...]
     spans = [slice(h * width, (h + 1) * width) for h in range(heads)]
     for step, pair_ref in enumerate(pair_refs):
@@ -59,12 +58,8 @@
         value_term = jnp.dot(
             jnp.concatenate(probs, axis=1), grads, preferred_element_type=jnp.float32
         )
-        for n, term in enumerate((key_term, value_term)):
-            for k in range(kv_count):
-                at = (n * kv_count + k) * width
-                terms_ref[mine - step, :, at : at + width] = jnp.where(
-                    kv_head == k, term, 0.0
-                ).astype(jnp.bfloat16)
+        terms_ref[mine - step, :, :width] = key_term.astype(jnp.bfloat16)
+        terms_ref[mine - step, :, width:] = value_term.astype(jnp.bfloat16)
 
     block(0, True)
 
@@ -109,7 +104,7 @@
         attention_kernel,
         out_shape=(
             jax.ShapeDtypeStruct(queries.shape, jnp.bfloat16),
-            jax.ShapeDtypeStruct((cycle, rows, 2 * kv_count * width), jnp.bfloat16),
+            jax.ShapeDtypeStruct((cycle, rows, 2 * width), jnp.bfloat16),
         ),
         in_specs=[scalars] * 2 + [whole] * (4 + cycle),
         out_specs=(whole, whole),
@@ -120,7 +115,7 @@
         compiler_params=pltpu.CompilerParams(vmem_limit_bytes=40 * 2**20),
         name="attention",
     )(
-        jnp.stack([mine, kv_head]).astype(jnp.int32),
+        mine.astype(jnp.int32)[None],
         block_mask,
         queries,
         attn_out_grad,
@@ -128,13 +123,43 @@
         lse_excess,
         *arrived,
     )
-    total = lax.psum_scatter(
-        terms.reshape(cycle * rows, 2 * kv_count * width),
+    return query_grad, terms
+
+
+def sum_kernel(parts_ref, key_ref, value_ref):
+    cycle, owners, rows, columns = parts_ref.shape
+    kv_count = key_ref.shape[1] * 2 // columns
+    group = owners // kv_count
+    width = columns // 2
+    for k in range(kv_count):
+        total = jnp.zeros((rows, columns), jnp.float32)
+        for c in range(cycle):
+            for e in range(k * group, (k + 1) * group):
+                total += parts_ref[c, e].astype(jnp.float32)
+        key_ref[:, k * width : (k + 1) * width] = total[:, :width].astype(jnp.bfloat16)
+        value_ref[:, k * width : (k + 1) * width] = total[:, width:].astype(jnp.bfloat16)
+
+
+def summed_terms(terms, kv_columns):
+    cycle, owners = lax.axis_size("ctx"), lax.axis_size("exp")
+    rows, columns = terms.shape[1] // owners, terms.shape[2]
+    parts = lax.all_to_all(
+        terms.reshape(cycle * owners, rows, columns),
         ("ctx", "exp"),
-        scatter_dimension=0,
+        split_axis=0,
+        concat_axis=0,
         tiled=True,
     )
-    return query_grad, total
+    whole = pl.BlockSpec(memory_space=pltpu.VMEM)
+    out = jax.ShapeDtypeStruct((rows, kv_columns), jnp.bfloat16)
+    return pl.pallas_call(
+        sum_kernel,
+        out_shape=(out, out),
+        in_specs=[whole],
+        out_specs=(whole, whole),
+        compiler_params=pltpu.CompilerParams(vmem_limit_bytes=40 * 2**20),
+        name="sums",
+    )(parts.reshape(cycle, owners, rows, columns))
 
 
 def weight_kernel(order_ref, flag_ref, probs_ref, hidden_ref, shadow_ref, weight_ref):
@@ -191,53 +216,52 @@
     )(order, flags, probs, hidden, shadow_rows)
 
 
-def tile_kernel(weight_ref, first_ref, second_ref, *rest):
-    tile_ref = rest[-1]
-    depth = first_ref.shape[0]
-    tile_ref[...] = jnp.dot(
-        weight_ref[:, :depth], first_ref[...], preferred_element_type=jnp.float32
-    ) + jnp.dot(weight_ref[:, depth:], second_ref[...], preferred_element_type=jnp.float32)
-
-
-def tile_columns(weighted, first, second, width, start, tiles):
-    depth, columns = first.shape
+def tile_kernel(start, count, weight_ref, *refs):
+    tile_ref = refs[-1]
+    blocks = jnp.concatenate([ref[...] for ref in refs[:count]], axis=0)
+    tile = jnp.dot(
+        weight_ref[:, start : start + blocks.shape[0]], blocks, preferred_element_type=jnp.float32
+    )
+    for ref in refs[count:-1]:
+        tile += ref[...]
+    tile_ref[...] = tile
+
+
+def tile_sum(weighted, blocks, start, partial):
+    tokens, model = blocks[0].shape
     rows = weighted.shape[0]
-    step = min(512, columns)
-    shift = start // step
-    gathered = pl.BlockSpec((depth, step), lambda i: (0, i))
-    earlier = [] if tiles is None else [tiles]
+    step = 512
+    column = lambda i: (0, i)
+    earlier = [] if partial is None else [partial]
+    depth = len(blocks) * tokens
     return pl.pallas_call(
-        tile_kernel,
-        out_shape=jax.ShapeDtypeStruct((rows, width), jnp.float32),
-        grid=(columns // step,),
-        in_specs=[pl.BlockSpec(weighted.shape, lambda i: (0, 0)), gathered, gathered]
-        + [pl.BlockSpec(memory_space=pl.ANY)] * len(earlier),
-        out_specs=pl.BlockSpec((rows, step), lambda i: (0, i + shift)),
-        input_output_aliases={3: 0} if earlier else {},
-        compiler_params=pltpu.CompilerParams(vmem_limit_bytes=40 * 2**20),
+        functools.partial(tile_kernel, start, len(blocks)),
+        out_shape=jax.ShapeDtypeStruct((rows, model), jnp.float32),
+        grid=(model // step,),
+        in_specs=[pl.BlockSpec(weighted.shape, lambda i: (0, 0))]
+        + [pl.BlockSpec((tokens, step), column)] * len(blocks)
+        + [pl.BlockSpec((rows, step), column)] * len(earlier),
+        out_specs=pl.BlockSpec((rows, step), column),
+        compiler_params=pltpu.CompilerParams(vmem_limit_bytes=50 * 2**20),
+        cost_estimate=pl.CostEstimate(
+            flops=2 * rows * depth * model,
+            bytes_accessed=4 * rows * model * (1 + len(earlier)) + 2 * depth * model,
+            transcendentals=0,
+        ),
         name="tiles",
-    )(weighted, first, second, *earlier)
-
-
-def experts(expert_ids, route_probs, moe_grad, shadow_list, stored_hidden_state):
+    )(weighted, *blocks, *earlier)
+
+
+def experts(expert_ids, route_probs, moe_grad, shadow_list, stored_hidden_state, anchor):
     owners = lax.axis_size("exp")
     own_index = lax.axis_index("exp")
+    swap = functools.partial(
+        lax.all_to_all, axis_name="exp", split_axis=0, concat_axis=0, tiled=True
+    )
     tokens, model = moe_grad.shape
     count = shadow_list.shape[0]
     per_dev = count // owners
     units = stored_hidden_state.shape[4]
-    chips = owners // 2
-    ring = [chip ^ (chip >> 1) for chip in range(chips)]
-    alike = [[2 * chip for chip in ring], [2 * chip + 1 for chip in ring[::-1]]]
-    swap = functools.partial(
-        lax.all_to_all, axis_name="exp", split_axis=0, concat_axis=0, tiled=True
-    )
-    parts = 2
-    gathered = [
-        lax.all_gather(columns, "exp", axis_index_groups=alike, tiled=True)
-        for columns in jnp.split(moe_grad, parts, axis=1)
-    ]
-
     hit = expert_ids[:, None, :] == jnp.arange(count, dtype=jnp.int32)[None, :, None]
     table = jnp.sum(
         jnp.where(hit, route_probs[:, None, :].astype(jnp.float32), 0.0), axis=2
@@ -255,32 +279,69 @@
     probs = mixed[:, limit:].reshape(owners, extra * units)[:, : per_dev * tokens]
     probs = probs.reshape(owners, per_dev, tokens)
     hosts = jnp.max(shadow_list.reshape(owners, per_dev), axis=1)
-    shadow_rows = swap(mixed[:, :limit][hosts])
+    sent, _ = lax.optimization_barrier((mixed[:, :limit][hosts], anchor))
+    shadow_rows = swap(sent)
     flags = lax.dynamic_slice_in_dim(shadow_list, own_index * per_dev, per_dev) >= 0
-    order = jnp.where(
-        own_index % 2 == 0,
-        jnp.array(alike[0] + alike[1], jnp.int32),
-        jnp.array(alike[1] + alike[0], jnp.int32),
+    steps = block_steps(owners)
+    orders = [
+        [step ^ turn for pair in zip(steps[core], steps[1 - core]) for step, turn in zip(pair, (0, 1))]
+        for core in range(2)
+    ]
+    order = own_index ^ jnp.where(
+        own_index % 2 == 0, jnp.array(orders[0], jnp.int32), jnp.array(orders[1], jnp.int32)
     )
     weighted = weighted_rows(
         probs, stored_hidden_state, shadow_rows, flags.astype(jnp.int32), order
     )
-    return weighted, gathered
-
-
-def expert_tiles(weighted, gathered, anchors, per_dev):
+    return weighted, probs
+
+
+def block_steps(owners):
+    masks = [1 << bit for bit in range(1, owners.bit_length() - 1)]
+    steps = []
+    for core in range(2):
+        first, second = masks[1 - core], masks[core]
+        held = [0, first, second, first ^ second]
+        for mask in masks[2:]:
+            held = held + [step ^ mask for step in held]
+        steps.append(held)
+    return steps
+
+
+def moved(value, steps):
     owners = lax.axis_size("exp")
-    model = sum(first.shape[1] for first in gathered)
-    pairs, second = [], None
-    for first, anchor in zip(gathered, anchors):
-        first, _ = lax.optimization_barrier((first, (anchor, second)))
-        second = lax.ppermute(first, "exp", [(e, e ^ 1) for e in range(owners)])
-        pairs.append((first, second))
-    tiles, start = None, 0
-    for first, second in pairs:
-        tiles = tile_columns(weighted, first, second, model, start, tiles)
-        start += first.shape[1]
-    return tiles.reshape(per_dev, weighted.shape[0] // per_dev, model)
+    return lax.ppermute(value, "exp", [(e, e ^ steps[e % 2]) for e in range(owners)])
+
+
+def near_blocks(moe_grad):
+    steps = block_steps(lax.axis_size("exp"))
+    first = moved(moe_grad, [held[1] for held in steps])
+    second = moved(moe_grad, [held[2] for held in steps])
+    return first, second, moved(moe_grad, (1, 1))
+
+
+def expert_tiles(weighted, moe_grad, near, anchor, per_dev):
+    owners = lax.axis_size("exp")
+    steps = block_steps(owners)
+    first, second, beside = near
+    first, _ = lax.optimization_barrier((first, anchor))
+    far = moved(first, [held[2] for held in steps])
+    second, _ = lax.optimization_barrier((second, anchor))
+    held = [moe_grad, first, second]
+    blocks = [moe_grad, beside] + [
+        block for part in held[1:] for block in (part, moved(part, (1, 1)))
+    ]
+    tiles = tile_sum(weighted, blocks, 0, None)
+    far, _ = lax.optimization_barrier((far, weighted))
+    held = held + [far]
+    rest = [far]
+    for turn in range(len(steps[0]).bit_length() - 3):
+        mask = steps[0][4 << turn]
+        more = [moved(part, (mask, mask)) for part in held]
+        held, rest = held + more, rest + more
+    rest = [block for part in rest for block in (part, moved(part, (1, 1)))]
+    tiles = tile_sum(weighted, rest, len(blocks) * moe_grad.shape[0], tiles)
+    return tiles.reshape(per_dev, weighted.shape[0] // per_dev, moe_grad.shape[1])
 
 
 def local(
@@ -297,16 +358,16 @@
     shadow_list,
     stored_hidden_state,
 ):
-    query_grad, kv_grad = attention(
+    near = near_blocks(moe_grad)
+    query_grad, terms = attention(
         queries, keys, values, attn_out, attn_out_grad, lse_excess, block_mask
     )
-    weighted, gathered = experts(
-        expert_ids, route_probs, moe_grad, shadow_list, stored_hidden_state
-    )
+    weighted, probs = experts(
+        expert_ids, route_probs, moe_grad, shadow_list, stored_hidden_state, query_grad
+    )
+    key_grad, value_grad = summed_terms(terms, keys.shape[1])
     per_dev = shadow_list.shape[0] // lax.axis_size("exp")
-    expert_grad = expert_tiles(weighted, gathered, ((weighted, query_grad), None), per_dev)
-    kv_grad, expert_grad = lax.optimization_barrier((kv_grad, expert_grad))
-    key_grad, value_grad = jnp.split(kv_grad, 2, axis=1)
+    expert_grad = expert_tiles(weighted, moe_grad, near, (query_grad, probs), per_dev)
     return (query_grad, key_grad, value_grad, expert_grad)
 
 

time: 221 us -> 102 us (0.46)
  waiting for transfers between devices: 155 us -> 30.1 us
  between operations: 15.9 us -> 0.97 us
  Pallas kernels: 21.3 us -> 32.8 us
  starting transfers between devices: 18.3 us -> 28.5 us
  local copies, waits for them, and re-layouts: 9.01 us -> 6.38 us
    reduce_scatter x1 -> x0, waiting for transfers between devices: 119 us -> none  [attention(): lax.psum_scatter(terms.reshape(cycle * rows, 2 * kv_count * width), ('ctx...]
    all_gather x2 -> x0, waiting for transfers between devices: 25.6 us -> none  [experts(): lax.all_gather(columns, 'exp', axis_index_groups=alike, tiled=True)]
    all_to_all x1 -> x2, waiting for transfers between devices: 7.51 us -> 23.1 us  [the longest x1 13.4 us: experts(): shadow_rows = swap(sent)]
    pallas_call x2 -> x3, Pallas kernels: 13.9 us -> 25.4 us  [the longest x2 24.7 us: tile_sum(): pl.pallas_call(functools.partial(tile_kernel, start, len(blocks)), out_sh...]
    ppermute x2 -> x7, starting transfers between devices: 0.11 us -> 6.79 us  [moved(): lax.ppermute(value, 'exp', [(e, e ^ steps[e % 2]) for e in range(owners)])]
    all_to_all x1 -> x2, starting transfers between devices: 3.45 us -> 8.96 us  [the longest x1 5.5 us: summed_terms(): lax.all_to_all(terms.reshape(cycle * owners, rows, columns), ('ctx', 'exp...]
    ppermute x3, waiting for transfers between devices: 0.01 us -> 4.91 us  [attention(): lax.ppermute(pair, 'ctx', [(c, c + step) for c in range(cycle - step)])]
    split x2 -> x0, local copies, waits for them, and re-layouts: 3.74 us -> none  [the longest x1 2.39 us: experts(): jnp.split(moe_grad, parts, axis=1)]
  transfers between devices with their start and end apart: 10 -> 13, of which waited for: 4 -> 5; matrix products, arithmetic and copies ran while one was open for 2% -> 5% of each run, Pallas kernels for 10% -> 20%
where the time goes in v4:
time: 102 us; the launch traced here: 101 us
  Pallas kernels  32.8 us (32%)
  waiting for transfers between devices  30.1 us (30%)
  starting transfers between devices  28.5 us (28%)
  local copies, waits for them, and re-layouts  6.38 us (6%)
  other arithmetic  2.45 us (2%)
    pallas_call x2, Pallas kernels, tile_sum(): pl.pallas_call(functools.partial(tile_kernel, start, len(blocks)), out_sh...  24.7 us
    all_to_all x1, waiting for transfers between devices, experts(): shadow_rows = swap(sent)  13.4 us
    all_to_all x1, waiting for transfers between devices, summed_terms(): lax.all_to_all(terms.reshape(cycle * owners, rows, columns), ('ctx', 'exp...  9.72 us
    ppermute x3, starting transfers between devices, attention(): lax.ppermute(pair, 'ctx', [(c, c + step) for c in range(cycle - step)])  9.29 us
    ppermute x7, starting transfers between devices, moved(): lax.ppermute(value, 'exp', [(e, e ^ steps[e % 2]) for e in range(owners)])  6.79 us
    all_to_all x1, starting transfers between devices, summed_terms(): lax.all_to_all(terms.reshape(cycle * owners, rows, columns), ('ctx', 'exp...  5.5 us
    ppermute x3, waiting for transfers between devices, attention(): lax.ppermute(pair, 'ctx', [(c, c + step) for c in range(cycle - step)])  4.91 us
    unnamed x30, local copies, waits for them, and re-layouts  4.81 us
  transfers between devices with their start and end apart: 13, of which 5 were waited for; matrix products, arithmetic and copies ran while one was open for 5% of the time, Pallas kernels for 20%

profile of v4, /device:TPU:0, one launch (start us, length us, event | category | flops | bytes accessed | tf_op | source)
XLA Modules:
  0.0 101.2 jit_solution(5028835575560551473)
XLA Ops:
  0.6 3.0 %collective-permute-start.3 = (bf16[128,4096]{1,0:T(8,128)(2,1)}, bf16[128,4096]{1,0:T(8,128)(2,1)}, u32[]{:S(2)}, u32[]{:S(2)}) collective-permute-start(bf16[128,4096]{1,0:T(8,128)(2,1)} %refs_0_.1), channel_id=1, source_target_pairs={{0,4},{1,3},{2,6},{3,1},{4,0},{5,7},{6,2},{7,5},{8,12},{9,11},{10,... | collective-permute-start | bytes 3145736 | tf_op jit(solution)/shard_map/ppermute | solution.py:313
  3.7 1.5 %collective-permute-start.8 = (bf16[128,4096]{1,0:T(8,128)(2,1)}, bf16[128,4096]{1,0:T(8,128)(2,1)}, u32[]{:S(2)}, u32[]{:S(2)}) collective-permute-start(bf16[128,4096]{1,0:T(8,128)(2,1)} %refs_0_.1), channel_id=1, source_target_pairs={{0,2},{1,5},{2,0},{3,7},{4,6},{5,1},{6,4},{7,3},{8,10},{9,13},{10,... | collective-permute-start | bytes 3145736 | tf_op jit(solution)/shard_map/ppermute | solution.py:313
  5.2 0.7 convert_element_type.17
  5.8 0.7 select_reduce_fusion
  6.6 1.5 %copy.30.hidden_ref = bf16[1,3,8,65,384]{4,3,2,1,0:T(8,128)(2,1)S(1)} copy(bf16[1,3,8,65,384]{4,2,3,1,0:T(8,128)(2,1)} %param.25) | data formatting | bytes 2396160 | tf_op args[11]
  8.1 0.0 copy-start.9
  8.1 0.0 copy-start.10
  8.1 0.0 copy-start.11
  8.1 0.0 copy-start.4
  8.1 0.0 copy-start.5
  8.1 0.0 copy-start.6
  8.1 0.0 copy-start.7
  8.1 0.0 copy-start.8
  8.2 0.8 pad_maximum_fusion
  9.0 3.5 %all-to-all-start.1 = ((bf16[8,65,384]{2,1,0:T(8,128)(2,1)}), bf16[8,65,384]{2,1,0:T(8,128)(2,1)S(1)}, u32[]{:S(2)}, u32[]{:S(2)}) async-start(bf16[8,65,384]{2,1,0:T(8,128)(2,1)} %pad_maximum_fusion), calls=%async_computation.1 | async-start | bytes 884736 | tf_op jit(solution)/shard_map/all_to_all | solution.py:273
  12.6 5.5 %collective-permute-start.2 = (bf16[256,256]{1,0:T(8,128)(2,1)S(1)}, bf16[256,256]{1,0:T(8,128)(2,1)S(1)}, u32[]{:S(2)}, u32[]{:S(2)}) collective-permute-start(bf16[256,256]{1,0:T(8,128)(2,1)S(1)} %pad_maximum_fusion.1.rest_0_), channel_id=1, source_target_pairs={{0,24},{1,25},{2,26},{3,27},{4,28},{5,29},{6,30},{7,31}} | collective-permute-start | bytes 393224 | tf_op jit(solution)/shard_map/ppermute | solution.py:98
  18.1 1.3 %collective-permute-start.1 = (bf16[256,256]{1,0:T(8,128)(2,1)S(1)}, bf16[256,256]{1,0:T(8,128)(2,1)S(1)}, u32[]{:S(2)}, u32[]{:S(2)}) collective-permute-start(bf16[256,256]{1,0:T(8,128)(2,1)S(1)} %pad_maximum_fusion.1.rest_0_), channel_id=1, source_target_pairs={{0,16},{8,24},{1,17},{9,25},{2,18},{10,26},{3,19},{11,27},{4,20},{... | collective-permute-start | bytes 393224 | tf_op jit(solution)/shard_map/ppermute | solution.py:98
  19.4 2.5 %collective-permute-start = (bf16[256,256]{1,0:T(8,128)(2,1)S(1)}, bf16[256,256]{1,0:T(8,128)(2,1)S(1)}, u32[]{:S(2)}, u32[]{:S(2)}) collective-permute-start(bf16[256,256]{1,0:T(8,128)(2,1)S(1)} %pad_maximum_fusion.1.rest_0_), channel_id=1, source_target_pairs={{0,8},{8,16},{16,24},{1,9},{9,17},{17,25},{2,10},{10,18},{18,26},{... | collective-permute-start | bytes 393224 | tf_op jit(solution)/shard_map/ppermute | solution.py:98
  21.9 0.1 reshape.54
  22.0 0.1 reduce_max.11
  22.1 0.0 collective-permute-done.2.rest_3_
  22.1 2.7 %collective-permute-done.1.rest_2_ = bf16[256,256]{1,0:T(8,128)(2,1)S(1)} collective-permute-done((bf16[256,256]{1,0:T(8,128)(2,1)S(1)}, bf16[256,256]{1,0:T(8,128)(2,1)S(1)}, u32[]{:S(2)}, u32[]{:S(2)}) %collective-permute-start.1) | collective-permute-done | bytes 131104 | tf_op jit(solution)/shard_map/ppermute | solution.py:98
  24.8 2.2 %collective-permute-done.rest_1_ = bf16[256,256]{1,0:T(8,128)(2,1)S(1)} collective-permute-done((bf16[256,256]{1,0:T(8,128)(2,1)S(1)}, bf16[256,256]{1,0:T(8,128)(2,1)S(1)}, u32[]{:S(2)}, u32[]{:S(2)}) %collective-permute-start) | collective-permute-done | bytes 131104 | tf_op jit(solution)/shard_map/ppermute | solution.py:98
  27.1 3.1 %attention.1 = (bf16[256,512]{1,0:T(8,128)(2,1)}, bf16[4,256,256]{2,1,0:T(8,128)(2,1)S(1)}) custom-call(s32[1]{0:T(128)} %bitcast.place_ref, s32[4,4]{1,0:T(4,128)S(1)} %copy-done.8, bf16[256,512]{1,0:T(8,128)(2,1)S(1)} %copy-done.4, bf16[256,512]{1,0:T(8,128)(2,1)S(1)} %copy-done.5, bf16[256,512]{1,0:T(8,128)(2,1)S(1)} %copy-done.6, ...), custom_call_target="tpu_custom_call" | custom-call | tf_op jit(solution)/shard_map/attention/pallas_call | solution.py:103
  30.1 0.8 copy-done.3
  31.0 2.0 %all-to-all-done.1 = bf16[8,65,384]{2,1,0:T(8,128)(2,1)S(1)} async-done(((bf16[8,65,384]{2,1,0:T(8,128)(2,1)}), bf16[8,65,384]{2,1,0:T(8,128)(2,1)S(1)}, u32[]{:S(2)}, u32[]{:S(2)}) %all-to-all-start.1) | async-done | bytes 399392 | tf_op jit(solution)/shard_map/all_to_all | solution.py:273
  33.1 0.9 collective-permute-start.4
  34.0 0.0 copy-start.12
  34.0 0.0 copy-start.13
  34.1 1.3 %gather_fusion = bf16[8,64,384]{2,1,0:T(8,128)(2,1)} fusion(bf16[8,64,384]{2,1,0:T(8,128)(2,1)S(1)} %slice.21, s32[1024]{0:T(1024)S(1)} %pad_clamp_fusion), kind=kCustom, calls=%fused_computation | custom fusion | bytes 786464 | tf_op jit(solution)/shard_map/gather | solution.py:282
  35.4 3.5 %all-to-all-start.2 = ((bf16[8,64,384]{2,1,0:T(8,128)(2,1)}), bf16[8,64,384]{2,1,0:T(8,128)(2,1)S(1)}, u32[]{:S(2)}, u32[]{:S(2)}) async-start(bf16[8,64,384]{2,1,0:T(8,128)(2,1)} %gather_fusion), calls=%async_computation.2 | async-start | bytes 786432 | tf_op jit(solution)/shard_map/all_to_all | solution.py:283
  38.9 0.6 collective-permute-start.6
  39.4 0.1 collective-permute-start.7
  39.5 0.0 collective-permute-done.8.refs_4_
  39.5 0.4 collective-permute-start.9
  40.0 13.4 %all-to-all-done.2.shadow_ref = bf16[8,64,384]{2,1,0:T(8,128)(2,1)S(1)} async-done(((bf16[8,64,384]{2,1,0:T(8,128)(2,1)}), bf16[8,64,384]{2,1,0:T(8,128)(2,1)S(1)}, u32[]{:S(2)}, u32[]{:S(2)}) %all-to-all-start.2) | async-done | bytes 393248 | tf_op jit(solution)/shard_map/all_to_all | solution.py:283
  53.4 5.5 %all-to-all-start = ((bf16[32,32,256]{2,1,0:T(8,128)(2,1)}), bf16[32,32,256]{2,1,0:T(8,128)(2,1)S(1)}, u32[]{:S(2)}, u32[]{:S(2)}) async-start(bf16[32,32,256]{2,1,0:T(8,128)(2,1)} %bitcast.19), calls=%async_computation | async-start | bytes 1048576 | tf_op jit(solution)/shard_map/all_to_all | solution.py:146
  58.9 0.1 compare_convert_fusion.flag_ref
  59.0 4.3 %weighted.1.weight_ref = bf16[768,1024]{1,0:T(8,128)(2,1)S(1)} custom-call(s32[8]{0:T(128)S(1)} %fusion.order_ref, s32[2]{0:T(128)S(1)} %compare_convert_fusion.flag_ref, bf16[8,2,128]{2,1,0:T(2,128)(2,1)S(1)} %reshape.53.probs_ref, bf16[1,3,8,65,384]{4,3,2,1,0:T(8,128)(2,1)S(1)} %copy.30.hidden_ref, bf16[8,64,384]{2,1,0:T(8,128)(2,1)S(1)} %all-to-all-done.2.shadow_ref), custom_call_target="tpu_custom_call" | custom-call | tf_op jit(solution)/shard_map/weighted/pallas_call | solution.py:196
  63.3 0.0 copy-start
  63.3 1.1 %copy-done = bf16[768,1024]{1,0:T(8,128)(2,1)} copy-done((bf16[768,1024]{1,0:T(8,128)(2,1)}, bf16[768,1024]{1,0:T(8,128)(2,1)S(1)}, u32[]{:S(2)}) %copy-start) | copy-done | bytes 1572888
  64.4 0.3 collective-permute-start.5
  64.7 9.7 %all-to-all-done = bf16[32,32,256]{2,1,0:T(8,128)(2,1)S(1)} async-done(((bf16[32,32,256]{2,1,0:T(8,128)(2,1)}), bf16[32,32,256]{2,1,0:T(8,128)(2,1)S(1)}, u32[]{:S(2)}, u32[]{:S(2)}) %all-to-all-start) | async-done | bytes 524320 | tf_op jit(solution)/shard_map/all_to_all | solution.py:146
  74.4 0.7 sums.1
  75.1 0.0 copy-start.2
  75.1 1.3 %copy-done.2 = bf16[128,4096]{1,0:T(8,128)(2,1)S(1)} copy-done((bf16[128,4096]{1,0:T(8,128)(2,1)S(1)}, bf16[128,4096]{1,0:T(8,128)(2,1)}, u32[]{:S(2)}) %copy-start.2) | copy-done | bytes 1048600
  76.5 12.4 %tiles.2.refs_2_ = f32[768,4096]{1,0:T(8,128)} custom-call(bf16[768,1024]{1,0:T(8,128)(2,1)} %copy-done, bf16[128,4096]{1,0:T(8,128)(2,1)S(1)} %copy-done.2, bf16[128,4096]{1,0:T(8,128)(2,1)} %collective-permute-done.6.refs_1_, bf16[128,4096]{1,0:T(8,128)(2,1)} %collective-permute-done.3.refs_2_, bf16[128,4096]{1,0:T(8,128)(2,1)} %collective-permute-done.7.refs_3_, ...), custom_call_target="tpu_custom_call" | custom-call | flops 4831838208 | bytes 18874368 | tf_op jit(solution)/shard_map/tiles/pallas_call | solution.py:237
  88.9 12.3 %tiles.3 = f32[768,4096]{1,0:T(8,128)} custom-call(bf16[768,1024]{1,0:T(8,128)(2,1)S(1)} %copy-done.1, bf16[128,4096]{1,0:T(8,128)(2,1)S(1)} %collective-permute-done.4.refs_0_, bf16[128,4096]{1,0:T(8,128)(2,1)S(1)} %collective-permute-done.5.refs_1_, f32[768,4096]{1,0:T(8,128)} %tiles.2.refs_2_), custom_call_target="tpu_custom_call" | custom-call | flops 1610612736 | bytes 27262976 | tf_op jit(solution)/shard_map/tiles/pallas_call | solution.py:237
  (33 shorter events, 0.2 us)
Async XLA Ops:
  0.6 32.4 %collective-permute-start.3 = (bf16[128,4096]{1,0:T(8,128)(2,1)}, bf16[128,4096]{1,0:T(8,128)(2,1)}, u32[]{:S(2)}, u32[]{:S(2)}) collective-permute-start(bf16[128,4096]{1,0:T(8,128)(2,1)} %refs_0_.1), channel_id=1, source_target_pairs={{0,4},{1,3},{2,6},{3,1},{4,0},{5,7},{6,2},{7,5},{8,12},{9,11},{10,... | collective-permute-start | bytes 3145736 | tf_op jit(solution)/shard_map/ppermute | solution.py:313
  3.7 35.9 %collective-permute-start.8 = (bf16[128,4096]{1,0:T(8,128)(2,1)}, bf16[128,4096]{1,0:T(8,128)(2,1)}, u32[]{:S(2)}, u32[]{:S(2)}) collective-permute-start(bf16[128,4096]{1,0:T(8,128)(2,1)} %refs_0_.1), channel_id=1, source_target_pairs={{0,2},{1,5},{2,0},{3,7},{4,6},{5,1},{6,4},{7,3},{8,10},{9,13},{10,... | collective-permute-start | bytes 3145736 | tf_op jit(solution)/shard_map/ppermute | solution.py:313
  8.1 4.5 %copy-start.9 = (bf16[256,256]{1,0:T(8,128)(2,1)S(1)}, bf16[256,256]{1,0:T(8,128)(2,1)}, u32[]{:S(2)}) copy-start(bf16[256,256]{1,0:T(8,128)(2,1)} %param.16) | copy-start | bytes 393220
  8.1 4.5 %copy-start.10 = (bf16[256,256]{1,0:T(8,128)(2,1)S(1)}, bf16[256,256]{1,0:T(8,128)(2,1)}, u32[]{:S(2)}) copy-start(bf16[256,256]{1,0:T(8,128)(2,1)} %param.15) | copy-start | bytes 393220
  8.1 13.8 %copy-start.11 = (s32[16]{0:T(128)S(1)}, s32[16]{0:T(128)}, u32[]{:S(2)}) copy-start(s32[16]{0:T(128)} %param.24) | copy-start | bytes 196
  8.1 18.9 %copy-start.4 = (bf16[256,512]{1,0:T(8,128)(2,1)S(1)}, bf16[256,512]{1,0:T(8,128)(2,1)}, u32[]{:S(2)}) copy-start(bf16[256,512]{1,0:T(8,128)(2,1)} %query_ref.1) | copy-start | bytes 786436
  8.1 18.9 %copy-start.5 = (bf16[256,512]{1,0:T(8,128)(2,1)S(1)}, bf16[256,512]{1,0:T(8,128)(2,1)}, u32[]{:S(2)}) copy-start(bf16[256,512]{1,0:T(8,128)(2,1)} %grad_ref.1) | copy-start | bytes 786436
  8.1 18.9 %copy-start.6 = (bf16[256,512]{1,0:T(8,128)(2,1)S(1)}, bf16[256,512]{1,0:T(8,128)(2,1)}, u32[]{:S(2)}) copy-start(bf16[256,512]{1,0:T(8,128)(2,1)} %out_ref.1) | copy-start | bytes 786436
  8.1 18.9 %copy-start.7 = (f32[4,256]{1,0:T(4,128)S(1)}, f32[4,256]{1,0:T(4,128)}, u32[]{:S(2)}) copy-start(f32[4,256]{1,0:T(4,128)} %lse_ref.1) | copy-start | bytes 12292
  8.1 18.9 %copy-start.8 = (s32[4,4]{1,0:T(4,128)S(1)}, s32[4,4]{1,0:T(4,128)}, u32[]{:S(2)}) copy-start(s32[4,4]{1,0:T(4,128)} %mask_ref.1) | copy-start | bytes 196
  9.0 24.0 %all-to-all-start.1 = ((bf16[8,65,384]{2,1,0:T(8,128)(2,1)}), bf16[8,65,384]{2,1,0:T(8,128)(2,1)S(1)}, u32[]{:S(2)}, u32[]{:S(2)}) async-start(bf16[8,65,384]{2,1,0:T(8,128)(2,1)} %pad_maximum_fusion), calls=%async_computation.1 | async-start | bytes 884736 | tf_op jit(solution)/shard_map/all_to_all | solution.py:273
  12.6 9.5 %collective-permute-start.2 = (bf16[256,256]{1,0:T(8,128)(2,1)S(1)}, bf16[256,256]{1,0:T(8,128)(2,1)S(1)}, u32[]{:S(2)}, u32[]{:S(2)}) collective-permute-start(bf16[256,256]{1,0:T(8,128)(2,1)S(1)} %pad_maximum_fusion.1.rest_0_), channel_id=1, source_target_pairs={{0,24},{1,25},{2,26},{3,27},{4,28},{5,29},{6,30},{7,31}} | collective-permute-start | bytes 393224 | tf_op jit(solution)/shard_map/ppermute | solution.py:98
  18.1 6.7 %collective-permute-start.1 = (bf16[256,256]{1,0:T(8,128)(2,1)S(1)}, bf16[256,256]{1,0:T(8,128)(2,1)S(1)}, u32[]{:S(2)}, u32[]{:S(2)}) collective-permute-start(bf16[256,256]{1,0:T(8,128)(2,1)S(1)} %pad_maximum_fusion.1.rest_0_), channel_id=1, source_target_pairs={{0,16},{8,24},{1,17},{9,25},{2,18},{10,26},{3,19},{11,27},{4,20},{... | collective-permute-start | bytes 393224 | tf_op jit(solution)/shard_map/ppermute | solution.py:98
  19.4 7.6 %collective-permute-start = (bf16[256,256]{1,0:T(8,128)(2,1)S(1)}, bf16[256,256]{1,0:T(8,128)(2,1)S(1)}, u32[]{:S(2)}, u32[]{:S(2)}) collective-permute-start(bf16[256,256]{1,0:T(8,128)(2,1)S(1)} %pad_maximum_fusion.1.rest_0_), channel_id=1, source_target_pairs={{0,8},{8,16},{16,24},{1,9},{9,17},{17,25},{2,10},{10,18},{18,26},{... | collective-permute-start | bytes 393224 | tf_op jit(solution)/shard_map/ppermute | solution.py:98
  30.1 0.8 copy-start.3
  33.1 31.4 %collective-permute-start.4 = (bf16[128,4096]{1,0:T(8,128)(2,1)}, bf16[128,4096]{1,0:T(8,128)(2,1)S(1)}, u32[]{:S(2)}, u32[]{:S(2)}) collective-permute-start(bf16[128,4096]{1,0:T(8,128)(2,1)} %collective-permute-done.3.refs_2_), channel_id=1, source_target_pairs={{0,2},{1,5},{2,0},{3,7},{4,6},{5,1},{6,4},{7,3},{8,10},{9,13},{10,... | collective-permute-start | bytes 3145736 | tf_op jit(solution)/shard_map/ppermute | solution.py:313
  34.0 25.0 %copy-start.12 = (s32[8]{0:T(128)S(1)}, s32[8]{0:T(128)}, u32[]{:S(2)}) copy-start(s32[8]{0:T(128)} %constant.57.clone) | copy-start | bytes 100
  34.0 25.0 %copy-start.13 = (s32[8]{0:T(128)S(1)}, s32[8]{0:T(128)}, u32[]{:S(2)}) copy-start(s32[8]{0:T(128)} %constant.56.clone) | copy-start | bytes 100
  35.4 17.9 %all-to-all-start.2 = ((bf16[8,64,384]{2,1,0:T(8,128)(2,1)}), bf16[8,64,384]{2,1,0:T(8,128)(2,1)S(1)}, u32[]{:S(2)}, u32[]{:S(2)}) async-start(bf16[8,64,384]{2,1,0:T(8,128)(2,1)} %gather_fusion), calls=%async_computation.2 | async-start | bytes 786432 | tf_op jit(solution)/shard_map/all_to_all | solution.py:283
  38.9 36.2 %collective-permute-start.6 = (bf16[128,4096]{1,0:T(8,128)(2,1)}, bf16[128,4096]{1,0:T(8,128)(2,1)}, u32[]{:S(2)}, u32[]{:S(2)}) collective-permute-start(bf16[128,4096]{1,0:T(8,128)(2,1)} %refs_0_.1), channel_id=1, source_target_pairs={{0,1},{1,0},{2,3},{3,2},{4,5},{5,4},{6,7},{7,6},{8,9},{9,8},{10,11... | collective-permute-start | bytes 3145736 | tf_op jit(solution)/shard_map/ppermute | solution.py:313
  39.4 35.7 %collective-permute-start.7 = (bf16[128,4096]{1,0:T(8,128)(2,1)}, bf16[128,4096]{1,0:T(8,128)(2,1)}, u32[]{:S(2)}, u32[]{:S(2)}) collective-permute-start(bf16[128,4096]{1,0:T(8,128)(2,1)} %collective-permute-done.3.refs_2_), channel_id=1, source_target_pairs={{0,1},{1,0},{2,3},{3,2},{4,5},{5,4},{6,7},{7,6},{8,9},{9,8},{10,11... | collective-permute-start | bytes 3145736 | tf_op jit(solution)/shard_map/ppermute | solution.py:313
  39.5 35.6 %collective-permute-start.9 = (bf16[128,4096]{1,0:T(8,128)(2,1)}, bf16[128,4096]{1,0:T(8,128)(2,1)}, u32[]{:S(2)}, u32[]{:S(2)}) collective-permute-start(bf16[128,4096]{1,0:T(8,128)(2,1)} %collective-permute-done.8.refs_4_), channel_id=1, source_target_pairs={{0,1},{1,0},{2,3},{3,2},{4,5},{5,4},{6,7},{7,6},{8,9},{9,8},{10,11... | collective-permute-start | bytes 3145736 | tf_op jit(solution)/shard_map/ppermute | solution.py:313
  53.4 21.1 %all-to-all-start = ((bf16[32,32,256]{2,1,0:T(8,128)(2,1)}), bf16[32,32,256]{2,1,0:T(8,128)(2,1)S(1)}, u32[]{:S(2)}, u32[]{:S(2)}) async-start(bf16[32,32,256]{2,1,0:T(8,128)(2,1)} %bitcast.19), calls=%async_computation | async-start | bytes 1048576 | tf_op jit(solution)/shard_map/all_to_all | solution.py:146
  63.3 1.1 %copy-start = (bf16[768,1024]{1,0:T(8,128)(2,1)}, bf16[768,1024]{1,0:T(8,128)(2,1)S(1)}, u32[]{:S(2)}) copy-start(bf16[768,1024]{1,0:T(8,128)(2,1)S(1)} %weighted.1.weight_ref) | copy-start | bytes 4718596
  64.4 24.5 %collective-permute-start.5 = (bf16[128,4096]{1,0:T(8,128)(2,1)S(1)}, bf16[128,4096]{1,0:T(8,128)(2,1)S(1)}, u32[]{:S(2)}, u32[]{:S(2)}) collective-permute-start(bf16[128,4096]{1,0:T(8,128)(2,1)S(1)} %collective-permute-done.4.refs_0_), channel_id=1, source_target_pairs={{0,1},{1,0},{2,3},{3,2},{4,5},{5,4},{6,7},{7,6},{8,9},{9,8},{10,11... | collective-permute-start | bytes 3145736 | tf_op jit(solution)/shard_map/ppermute | solution.py:313
  75.1 13.8 %copy-start.1 = (bf16[768,1024]{1,0:T(8,128)(2,1)S(1)}, bf16[768,1024]{1,0:T(8,128)(2,1)}, u32[]{:S(2)}) copy-start(bf16[768,1024]{1,0:T(8,128)(2,1)} %copy-done) | copy-start | bytes 4718596
  75.1 1.3 %copy-start.2 = (bf16[128,4096]{1,0:T(8,128)(2,1)S(1)}, bf16[128,4096]{1,0:T(8,128)(2,1)}, u32[]{:S(2)}) copy-start(bf16[128,4096]{1,0:T(8,128)(2,1)} %refs_0_.1) | copy-start | bytes 3145732
